TPU v7x, 512 devices: a whole 4x4x16 slice. The times are simulated.
512 devices in a mesh: patch: 2 (over core), lat: 64 (over z, y), rad: 4 (over x).
Axes of the slice: x: 4, y: 4, z: 16, core: 2. Of those that a mesh axis runs over, the one named last changes fastest.
Arguments:
- iterate_in: float32 [2, 4, 8, 1024, 256], P('patch', None, 'rad', 'lat'), may hold values from -6 to 6
- forcing: float32 [2, 4, 8, 1024, 256], P('patch', None, 'rad', 'lat'), may hold values from -6 to 6
- viscosity: float32 [2, 8, 1024, 256], P('patch', 'rad', 'lat'), may hold values from 0.1 to 10
- vanka_inverse: float32 [2, 4, 4, 8, 1024, 256], P('patch', None, None, 'rad', 'lat'), may hold values from -1 to 2, as said below
- pack_cells: int32 [2, 64, 64, 4], P('patch', 'lat'), may hold values from 0 to 4095
- take_slot: int32 [2, 64, 32, 4], P('patch', 'lat'), may hold values from 0 to 255, as said below
- take_weight: float32 [2, 64, 32, 4], P('patch', 'lat'), may hold values from 0.1 to 0.4
Outputs:
- iterate: float32 [2, 4, 8, 1024, 256], P('patch', None, 'rad', 'lat')
- coarse_correction: float32 [2, 4, 4, 512, 128], P('patch', None, 'rad', 'lat')
Inputs may be any that keep to these rules, and one draw needn't show every extreme that they name: `take_slot`: A slot s names source strip s // 4, which lies among the 32 strips starting at the destination strip minus 32 // 2, cyclically. `vanka_inverse`: symmetric per cell.
All inputs are finite; a program needn't handle non-finite values.
Results may differ from a plain program's by a relative error of at most 0.0001.
Values sent between devices are 32-bit elements; how exact they have to be, the bound alone decides.
A program may use at most 64 MiB of HBM per device.

v0:
```python
import jax
import jax.numpy as jnp
from jax import lax
from jax.sharding import PartitionSpec as P

SWEEPS = 3


OMEGA = 0.8


def padded_2(block, sides, width):
    for axis, dim in sides:
        count = lax.axis_size(axis)
        forward = [(i, i + 1) for i in range(count - 1)]
        backward = [(target, source) for source, target in forward]
        low = lax.ppermute(
            lax.slice_in_dim(block, block.shape[dim] - width, None, axis=dim), axis, forward
        )
        high = lax.ppermute(lax.slice_in_dim(block, 0, width, axis=dim), axis, backward)
        block = jnp.concatenate([low, block, high], axis=dim)
    return block


def interior(array, spatial, offset):
    picks = [slice(1, -1), slice(1, -1), slice(1, -1)]
    picks[spatial] = slice(2, None) if offset > 0 else slice(0, -2)
    leading = (slice(None),) * (array.ndim - 3)
    return array[leading + tuple(picks)]


def operate(padded, viscous, lap_scale, grad_scale):
    centre = padded[:, 1:-1, 1:-1, 1:-1]
    middle = viscous[1:-1, 1:-1, 1:-1]
    friction = jnp.zeros_like(centre[:3])
    pressure_sum = jnp.zeros_like(middle)
    divergence = jnp.zeros_like(middle)
    gradients = []
    for spatial in range(3):
        upper_cell = interior(padded, spatial, 1)
        lower_cell = interior(padded, spatial, -1)
        upper_face = 0.5 * (middle + interior(viscous, spatial, 1))
        lower_face = 0.5 * (middle + interior(viscous, spatial, -1))
        friction = (
            friction
            + upper_face * (centre[:3] - upper_cell[:3])
            + lower_face * (centre[:3] - lower_cell[:3])
        )
        pressure_sum = pressure_sum + upper_cell[3] + lower_cell[3]
        gradients.append(0.5 * (upper_cell[3] - lower_cell[3]))
        divergence = divergence + 0.5 * (upper_cell[spatial] - lower_cell[spatial])
    velocity = lap_scale * friction + grad_scale * jnp.stack(gradients)
    pressure = lap_scale * (6.0 * centre[3] - pressure_sum) / middle - grad_scale * divergence
    return jnp.concatenate([velocity, pressure[None]], axis=0)


def diagonal(viscous, lap_scale):
    middle = viscous[1:-1, 1:-1, 1:-1]
    faces = jnp.zeros_like(middle)
    for spatial in range(3):
        for offset in (1, -1):
            faces = faces + 0.5 * (middle + interior(viscous, spatial, offset))
    return lap_scale * jnp.stack([faces, faces, faces, 6.0 / middle])


def restrict(field):
    shape = field.shape
    lead = shape[:-3]
    blocks = field.reshape(lead + (shape[-3] // 2, 2, shape[-2] // 2, 2, shape[-1] // 2, 2))
    count = len(lead)
    return jnp.mean(blocks, axis=(count + 1, count + 3, count + 5))


def edge_latitude(padded):
    return jnp.pad(padded, ((0, 0), (0, 0), (1, 1)), mode="edge")


def shards(iterate_in, forcing, viscosity, vanka_inverse, pack_cells, take_slot, take_weight):
    iterate = iterate_in[0]
    forcing_local = forcing[0]
    visc_local = viscosity[0]
    inverse = vanka_inverse[0]
    cells = pack_cells[0, 0]
    slots = take_slot[0, 0]
    weights = take_weight[0, 0]
    radial = iterate.shape[1]
    strip_width = iterate.shape[2]
    latitude = iterate.shape[3]
    capacity = cells.shape[1]
    strip_count = lax.axis_size("lat")
    fine_visc = edge_latitude(padded_2(visc_local, (("lat", 1), ("rad", 0)), 1))
    coarse_eta = padded_2(restrict(visc_local), (("lat", 1), ("rad", 0)), 1)
    coarse_visc = edge_latitude(coarse_eta)

    def rim_ghosts(field):
        flat = field.reshape(4, radial, strip_width * latitude)
        picked = jnp.take(flat, cells.reshape(-1), axis=2).reshape(4, radial, strip_count, capacity)
        outgoing = jnp.transpose(picked, (2, 0, 1, 3))
        own_patch = lax.axis_index("patch")
        blank = jnp.zeros_like(outgoing)
        doubled = jnp.where(
            own_patch == 0,
            jnp.concatenate([blank, outgoing], axis=0),
            jnp.concatenate([outgoing, blank], axis=0),
        )
        received = lax.all_to_all(
            doubled, ("patch", "lat"), split_axis=0, concat_axis=0, tiled=True
        )
        arrived = jnp.where(own_patch == 0, received[strip_count:], received[:strip_count])
        slab = jnp.transpose(arrived, (1, 2, 0, 3)).reshape(4, radial, strip_count * capacity)
        values = jnp.take(slab, slots.reshape(-1), axis=2).reshape(4, radial, 2 * strip_width, 4)
        ghosts = jnp.sum(values * weights, axis=-1)
        return (ghosts[..., :strip_width], ghosts[..., strip_width:])

    def fine_residual(field):
        middle = padded_2(field, (("lat", 2), ("rad", 1)), 1)
        lower, upper = rim_ghosts(field)
        lower_pad = jnp.pad(lower, ((0, 0), (1, 1), (1, 1)))[..., None]
        upper_pad = jnp.pad(upper, ((0, 0), (1, 1), (1, 1)))[..., None]
        padded = jnp.concatenate([lower_pad, middle, upper_pad], axis=3)
        return forcing_local - operate(padded, fine_visc, 1.0, 1.0)

    for sweep in range(SWEEPS):
        residual = fine_residual(iterate)
        iterate = iterate + OMEGA * jnp.sum(inverse * residual[None], axis=1)
    coarse_residual = restrict(fine_residual(iterate))
    scaling = diagonal(coarse_visc, 0.25)
    first = OMEGA * coarse_residual / scaling
    haloed = padded_2(first, (("lat", 2), ("rad", 1)), 1)
    padded = jnp.pad(haloed, ((0, 0), (0, 0), (0, 0), (1, 1)))
    second = first + OMEGA * (coarse_residual - operate(padded, coarse_visc, 0.25, 0.5)) / scaling
    return (iterate[None], second[None])


def solution(mesh):
    in_specs = (
        P("patch", None, "rad", "lat", None),
        P("patch", None, "rad", "lat", None),
        P("patch", "rad", "lat", None),
        P("patch", None, None, "rad", "lat", None),
        P("patch", "lat", None, None),
        P("patch", "lat", None, None),
        P("patch", "lat", None, None),
    )
    out_specs = (P("patch", None, "rad", "lat", None), P("patch", None, "rad", "lat", None))
    return jax.shard_map(shards, mesh=mesh, in_specs=in_specs, out_specs=out_specs, check_vma=False)
```

profile of v0, /device:TPU:1, one launch (start us, length us, event | category | flops | bytes accessed | tf_op | source)
XLA Modules:
  0.0 312.5 jit_solution(1386104072254759561)
XLA Ops:
  0.6 0.8 copy.547
  1.6 4.2 %copy.548 = f32[1,4,2,16,256]{1,2,4,3,0:T(2,128)} copy(f32[1,4,2,16,256]{4,3,2,1,0:T(8,128)} %param.11) | data formatting | bytes 262144 | tf_op args[0]
  5.8 3.2 %gather_fusion = f32[256,4,2]{1,2,0:T(2,128)S(1)} fusion(f32[4,2,4096]{0,1,2:T(2,128)} %bitcast.190, s32[1024]{0:T(1024)S(1)} %pad_clamp_fusion.1), kind=kCustom, calls=%fused_computation.clone | custom fusion | bytes 17408 | tf_op jit(solution)/shard_map/jit(_take)/gather | solution.py:97
  9.3 1.0 copy.601
  10.4 1.2 copy.550
  11.6 20.9 %all-to-all-start = ((f32[128,4,2,4]{3,2,1,0:T(2,128)}), f32[128,4,2,4]{3,2,1,0:T(2,128)S(1)}, u32[]{:S(2)}, u32[]{:S(2)}) async-start(f32[128,4,2,4]{3,2,1,0:T(2,128)} %copy.550), calls=%async_computation | async-start | bytes 1048576 | tf_op jit(solution)/shard_map/all_to_all | solution.py:106
  32.6 1.3 collective-permute-start.4
  33.9 4.0 %collective-permute-start.3 = (f32[4,2,1,256]{3,2,1,0:T(1,128)S(1)}, f32[4,2,1,256]{3,2,1,0:T(1,128)S(1)}, u32[]{:S(2)}, u32[]{:S(2)}) collective-permute-start(f32[4,2,1,256]{3,2,1,0:T(1,128)S(1)} %get-tuple-element.59), channel_id=1, source_target_pairs={{0,4},{4,8},{8,12},{12,16},{16,20},{20,24},{24,28},{28,32},{32,36}... | collective-permute-start | bytes 24584 | tf_op jit(solution)/shard_map/ppermute | solution.py:17
  37.9 1.3 collective-permute-start.1
  39.2 1.0 reduce_sum.106
  40.4 1.3 collective-permute-start.21
  41.7 4.6 %collective-permute-start.20 = (f32[1,1,128]{2,1,0:T(1,128)S(1)}, f32[1,1,128]{2,1,0:T(1,128)S(1)}, u32[]{:S(2)}, u32[]{:S(2)}) collective-permute-start(f32[1,1,128]{2,1,0:T(1,128)S(1)} %get-tuple-element.92), channel_id=1, source_target_pairs={{0,4},{4,8},{8,12},{12,16},{16,20},{20,24},{24,28},{28,32},{32,36}... | collective-permute-start | bytes 1544 | tf_op jit(solution)/shard_map/ppermute | solution.py:17
  46.7 3.4 %collective-permute-start = (f32[2,1,256]{2,1,0:T(1,128)S(1)}, f32[2,1,256]{2,1,0:T(1,128)S(1)}, u32[]{:S(2)}, u32[]{:S(2)}) collective-permute-start(f32[2,1,256]{2,1,0:T(1,128)S(1)} %get-tuple-element.73), channel_id=1, source_target_pairs={{0,4},{4,8},{8,12},{12,16},{16,20},{20,24},{24,28},{28,32},{32,36}... | collective-permute-start | bytes 6152 | tf_op jit(solution)/shard_map/ppermute | solution.py:17
  50.1 1.3 collective-permute-start.22
  51.4 4.0 %collective-permute-start.23 = (f32[1,10,128]{2,1,0:T(8,128)S(1)}, f32[1,10,128]{2,1,0:T(8,128)S(1)}, u32[]{:S(2)}, u32[]{:S(2)}) collective-permute-start(f32[1,10,128]{2,1,0:T(8,128)S(1)} %pad_maximum_fusion.95), channel_id=1, source_target_pairs={{0,1},{1,2},{2,3},{4,5},{5,6},{6,7},{8,9},{9,10},{10,11},{12,13},{... | collective-permute-start | bytes 15368 | tf_op jit(solution)/shard_map/ppermute | solution.py:17
  55.5 1.3 collective-permute-start.2
  56.8 4.0 %collective-permute-start.6 = (f32[1,18,256]{2,1,0:T(8,128)S(1)}, f32[1,18,256]{2,1,0:T(8,128)S(1)}, u32[]{:S(2)}, u32[]{:S(2)}) collective-permute-start(f32[1,18,256]{2,1,0:T(8,128)S(1)} %get-tuple-element.68), channel_id=1, source_target_pairs={{0,1},{1,2},{2,3},{4,5},{5,6},{6,7},{8,9},{9,10},{10,11},{12,13},{... | collective-permute-start | bytes 55304 | tf_op jit(solution)/shard_map/ppermute | solution.py:17
  61.1 1.4 collective-permute-start.5
  62.5 4.0 %collective-permute-start.7 = (f32[4,1,18,256]{3,2,1,0:T(8,128)S(1)}, f32[4,1,18,256]{3,2,1,0:T(8,128)S(1)}, u32[]{:S(2)}, u32[]{:S(2)}) collective-permute-start(f32[4,1,18,256]{3,2,1,0:T(8,128)S(1)} %get-tuple-element.29), channel_id=1, source_target_pairs={{0,1},{1,2},{2,3},{4,5},{5,6},{6,7},{8,9},{9,10},{10,11},{12,13},{... | collective-permute-start | bytes 221192 | tf_op jit(solution)/shard_map/ppermute | solution.py:17
  66.8 0.7 all-to-all-done
  67.7 0.9 copy.602
  68.5 0.7 gather_fusion.1
  71.4 3.1 %copy.557 = f32[4,2,16,256]{0,1,3,2:T(2,128)} copy(f32[4,2,16,256]{3,2,1,0:T(8,128)S(1)} %get-tuple-element.58) | data formatting | bytes 262144 | tf_op jit(solution)/shard_map/mul | solution.py:125
  74.6 6.6 %bitcast_add_fusion.2 = f32[4,2,4096]{0,1,2:T(2,128)} fusion(f32[4,2,16,256]{0,1,3,2:T(2,128)} %copy.557, f32[1,4,2,16,256]{1,2,4,3,0:T(2,128)} %copy.548), kind=kLoop, calls=%fused_computation.10 | loop fusion | flops 32768 | bytes 393216 | tf_op jit(solution)/shard_map/add | solution.py:125
  81.2 3.2 %gather_fusion.2 = f32[256,4,2]{1,2,0:T(2,128)S(1)} fusion(f32[4,2,4096]{0,1,2:T(2,128)} %bitcast_add_fusion.2, s32[1024]{0:T(1024)S(1)} %pad_clamp_fusion.1), kind=kCustom, calls=%fused_computation.2.clone | custom fusion | bytes 17408 | tf_op jit(solution)/shard_map/jit(_take)/gather | solution.py:97
  84.7 1.0 copy.604
  85.8 1.3 collective-permute-start.9
  87.1 4.5 %collective-permute-start.8 = (f32[4,2,1,256]{3,2,1,0:T(1,128)S(1)}, f32[4,2,1,256]{3,2,1,0:T(1,128)S(1)}, u32[]{:S(2)}, u32[]{:S(2)}) collective-permute-start(f32[4,2,1,256]{3,2,1,0:T(1,128)S(1)} %get-tuple-element.55), channel_id=1, source_target_pairs={{0,4},{4,8},{8,12},{12,16},{16,20},{20,24},{24,28},{28,32},{32,36}... | collective-permute-start | bytes 24584 | tf_op jit(solution)/shard_map/ppermute | solution.py:17
  91.6 1.2 copy.559
  92.8 28.4 %all-to-all-start.1 = ((f32[128,4,2,4]{3,2,1,0:T(2,128)}), f32[128,4,2,4]{3,2,1,0:T(2,128)S(1)}, u32[]{:S(2)}, u32[]{:S(2)}) async-start(f32[128,4,2,4]{3,2,1,0:T(2,128)} %copy.559), calls=%async_computation.1 | async-start | bytes 1048576 | tf_op jit(solution)/shard_map/all_to_all | solution.py:106
  121.3 1.3 collective-permute-start.10
  122.6 4.0 %collective-permute-start.11 = (f32[4,1,18,256]{3,2,1,0:T(8,128)S(1)}, f32[4,1,18,256]{3,2,1,0:T(8,128)S(1)}, u32[]{:S(2)}, u32[]{:S(2)}) collective-permute-start(f32[4,1,18,256]{3,2,1,0:T(8,128)S(1)} %get-tuple-element.27), channel_id=1, source_target_pairs={{0,1},{1,2},{2,3},{4,5},{5,6},{6,7},{8,9},{9,10},{10,11},{12,13},{... | collective-permute-start | bytes 221192 | tf_op jit(solution)/shard_map/ppermute | solution.py:17
  126.6 29.6 %all-to-all-done.1 = f32[128,4,2,4]{3,2,1,0:T(2,128)S(1)} async-done(((f32[128,4,2,4]{3,2,1,0:T(2,128)}), f32[128,4,2,4]{3,2,1,0:T(2,128)S(1)}, u32[]{:S(2)}, u32[]{:S(2)}) %all-to-all-start.1) | async-done | bytes 16416 | tf_op jit(solution)/shard_map/all_to_all | solution.py:106
  156.3 0.9 copy.605
  160.1 3.2 %copy.565 = f32[4,2,16,256]{0,1,3,2:T(2,128)} copy(f32[4,2,16,256]{3,2,1,0:T(8,128)S(1)} %get-tuple-element.54) | data formatting | bytes 262144 | tf_op jit(solution)/shard_map/mul | solution.py:125
  163.3 6.6 %bitcast_add_fusion.1 = f32[4,2,4096]{0,1,2:T(2,128)} fusion(f32[4,2,4096]{0,1,2:T(2,128)} %bitcast_add_fusion.2, f32[4,2,16,256]{0,1,3,2:T(2,128)} %copy.565), kind=kLoop, calls=%fused_computation.9 | loop fusion | flops 32768 | bytes 393216 | tf_op jit(solution)/shard_map/add | solution.py:125
  169.9 3.2 %gather_fusion.4 = f32[256,4,2]{1,2,0:T(2,128)S(1)} fusion(f32[4,2,4096]{0,1,2:T(2,128)} %bitcast_add_fusion.1, s32[1024]{0:T(1024)S(1)} %pad_clamp_fusion.1), kind=kCustom, calls=%fused_computation.3.clone | custom fusion | bytes 17408 | tf_op jit(solution)/shard_map/jit(_take)/gather | solution.py:97
  173.5 1.0 copy.607
  174.5 1.3 collective-permute-start.13
  175.8 4.0 %collective-permute-start.12 = (f32[4,2,1,256]{3,2,1,0:T(1,128)S(1)}, f32[4,2,1,256]{3,2,1,0:T(1,128)S(1)}, u32[]{:S(2)}, u32[]{:S(2)}) collective-permute-start(f32[4,2,1,256]{3,2,1,0:T(1,128)S(1)} %get-tuple-element.51), channel_id=1, source_target_pairs={{0,4},{4,8},{8,12},{12,16},{16,20},{20,24},{24,28},{28,32},{32,36}... | collective-permute-start | bytes 24584 | tf_op jit(solution)/shard_map/ppermute | solution.py:17
  179.9 1.2 copy.567
  181.1 8.4 %all-to-all-start.2 = ((f32[128,4,2,4]{3,2,1,0:T(2,128)}), f32[128,4,2,4]{3,2,1,0:T(2,128)S(1)}, u32[]{:S(2)}, u32[]{:S(2)}) async-start(f32[128,4,2,4]{3,2,1,0:T(2,128)} %copy.567), calls=%async_computation.2 | async-start | bytes 1048576 | tf_op jit(solution)/shard_map/all_to_all | solution.py:106
  189.5 1.3 collective-permute-start.14
  190.8 4.0 %collective-permute-start.15 = (f32[4,1,18,256]{3,2,1,0:T(8,128)S(1)}, f32[4,1,18,256]{3,2,1,0:T(8,128)S(1)}, u32[]{:S(2)}, u32[]{:S(2)}) collective-permute-start(f32[4,1,18,256]{3,2,1,0:T(8,128)S(1)} %get-tuple-element.25), channel_id=1, source_target_pairs={{0,1},{1,2},{2,3},{4,5},{5,6},{6,7},{8,9},{9,10},{10,11},{12,13},{... | collective-permute-start | bytes 221192 | tf_op jit(solution)/shard_map/ppermute | solution.py:17
  194.8 29.6 %all-to-all-done.2 = f32[128,4,2,4]{3,2,1,0:T(2,128)S(1)} async-done(((f32[128,4,2,4]{3,2,1,0:T(2,128)}), f32[128,4,2,4]{3,2,1,0:T(2,128)S(1)}, u32[]{:S(2)}, u32[]{:S(2)}) %all-to-all-start.2) | async-done | bytes 16416 | tf_op jit(solution)/shard_map/all_to_all | solution.py:106
  224.6 0.9 copy.608
  228.4 3.2 %copy.573 = f32[4,2,16,256]{0,1,3,2:T(2,128)} copy(f32[4,2,16,256]{3,2,1,0:T(8,128)S(1)} %get-tuple-element.50) | data formatting | bytes 262144 | tf_op jit(solution)/shard_map/mul | solution.py:125
  231.6 6.6 %bitcast_add_fusion = f32[4,2,4096]{0,1,2:T(2,128)} fusion(f32[4,2,4096]{0,1,2:T(2,128)} %bitcast_add_fusion.1, f32[4,2,16,256]{0,1,3,2:T(2,128)} %copy.573), kind=kLoop, calls=%fused_computation.8 | loop fusion | flops 32768 | bytes 393216 | tf_op jit(solution)/shard_map/add | solution.py:125
  238.2 3.2 %gather_fusion.6 = f32[256,4,2]{1,2,0:T(2,128)S(1)} fusion(f32[4,2,4096]{0,1,2:T(2,128)} %bitcast_add_fusion, s32[1024]{0:T(1024)S(1)} %pad_clamp_fusion.1), kind=kCustom, calls=%fused_computation.4.clone | custom fusion | bytes 17408 | tf_op jit(solution)/shard_map/jit(_take)/gather | solution.py:97
  241.7 1.0 copy.610
  242.8 1.3 collective-permute-start.17
  244.1 4.0 %collective-permute-start.16 = (f32[4,2,1,256]{3,2,1,0:T(1,128)S(1)}, f32[4,2,1,256]{3,2,1,0:T(1,128)S(1)}, u32[]{:S(2)}, u32[]{:S(2)}) collective-permute-start(f32[4,2,1,256]{3,2,1,0:T(1,128)S(1)} %get-tuple-element.47), channel_id=1, source_target_pairs={{0,4},{4,8},{8,12},{12,16},{16,20},{20,24},{24,28},{28,32},{32,36}... | collective-permute-start | bytes 24584 | tf_op jit(solution)/shard_map/ppermute | solution.py:17
  248.1 1.2 copy.575
  249.3 8.6 %all-to-all-start.3 = ((f32[128,4,2,4]{3,2,1,0:T(2,128)}), f32[128,4,2,4]{3,2,1,0:T(2,128)S(1)}, u32[]{:S(2)}, u32[]{:S(2)}) async-start(f32[128,4,2,4]{3,2,1,0:T(2,128)} %copy.575), calls=%async_computation.3 | async-start | bytes 1048576 | tf_op jit(solution)/shard_map/all_to_all | solution.py:106
  258.0 1.3 collective-permute-start.18
  259.3 4.0 %collective-permute-start.19 = (f32[4,1,18,256]{3,2,1,0:T(8,128)S(1)}, f32[4,1,18,256]{3,2,1,0:T(8,128)S(1)}, u32[]{:S(2)}, u32[]{:S(2)}) collective-permute-start(f32[4,1,18,256]{3,2,1,0:T(8,128)S(1)} %get-tuple-element.23), channel_id=1, source_target_pairs={{0,1},{1,2},{2,3},{4,5},{5,6},{6,7},{8,9},{9,10},{10,11},{12,13},{... | collective-permute-start | bytes 221192 | tf_op jit(solution)/shard_map/ppermute | solution.py:17
  263.3 29.6 %all-to-all-done.3 = f32[128,4,2,4]{3,2,1,0:T(2,128)S(1)} async-done(((f32[128,4,2,4]{3,2,1,0:T(2,128)}), f32[128,4,2,4]{3,2,1,0:T(2,128)S(1)}, u32[]{:S(2)}, u32[]{:S(2)}) %all-to-all-start.3) | async-done | bytes 16416 | tf_op jit(solution)/shard_map/all_to_all | solution.py:106
  293.1 0.9 copy.611
  297.5 1.7 reduce_sum.104
  299.4 1.3 collective-permute-start.25
  300.7 4.0 %collective-permute-start.24 = (f32[4,1,1,128]{3,2,0,1:T(1,128)S(1)}, f32[4,1,1,128]{3,2,0,1:T(1,128)S(1)}, u32[]{:S(2)}, u32[]{:S(2)}) collective-permute-start(f32[4,1,1,128]{3,2,0,1:T(1,128)S(1)} %get-tuple-element.81), channel_id=1, source_target_pairs={{0,4},{4,8},{8,12},{12,16},{16,20},{20,24},{24,28},{28,32},{32,36}... | collective-permute-start | bytes 6152 | tf_op jit(solution)/shard_map/ppermute | solution.py:17
  305.4 1.3 collective-permute-start.26
  306.7 4.0 %collective-permute-start.27 = (f32[4,1,10,128]{3,0,2,1:T(4,128)S(1)}, f32[4,1,10,128]{3,0,2,1:T(4,128)S(1)}, u32[]{:S(2)}, u32[]{:S(2)}) collective-permute-start(f32[4,1,10,128]{3,0,2,1:T(4,128)S(1)} %pad_maximum_fusion.94), channel_id=1, source_target_pairs={{0,1},{1,2},{2,3},{4,5},{5,6},{6,7},{8,9},{9,10},{10,11},{12,13},{... | collective-permute-start | bytes 61448 | tf_op jit(solution)/shard_map/ppermute | solution.py:17
  310.8 0.9 collective-permute-done.27
  (171 shorter events, 16.5 us)
Async XLA Ops:
  0.6 31.9 %copy-start = (f32[1,4,2,16,256]{4,3,2,1,0:T(8,128)S(1)}, f32[1,4,2,16,256]{4,3,2,1,0:T(8,128)}, u32[]{:S(2)}) copy-start(f32[1,4,2,16,256]{4,3,2,1,0:T(8,128)} %param.11) | copy-start | bytes 393220
  1.4 36.4 %copy-start.2 = (f32[1,2,16,256]{3,2,1,0:T(8,128)S(1)}, f32[1,2,16,256]{3,2,1,0:T(8,128)}, u32[]{:S(2)}) copy-start(f32[1,2,16,256]{3,2,1,0:T(8,128)} %param.13) | copy-start | bytes 98308
  1.6 44.8 %copy-start.4 = (s32[1,1,32,4]{2,3,1,0:T(4,128)S(1)}, s32[1,1,32,4]{2,3,1,0:T(4,128)}, u32[]{:S(2)}) copy-start(s32[1,1,32,4]{2,3,1,0:T(4,128)} %param.16) | copy-start | bytes 1540
  5.8 40.8 %copy-start.5 = (f32[1,1,32,4]{2,3,1,0:T(4,128)S(1)}, f32[1,1,32,4]{2,3,1,0:T(4,128)}, u32[]{:S(2)}) copy-start(f32[1,1,32,4]{2,3,1,0:T(4,128)} %param.17) | copy-start | bytes 1540
  11.6 55.9 %all-to-all-start = ((f32[128,4,2,4]{3,2,1,0:T(2,128)}), f32[128,4,2,4]{3,2,1,0:T(2,128)S(1)}, u32[]{:S(2)}, u32[]{:S(2)}) async-start(f32[128,4,2,4]{3,2,1,0:T(2,128)} %copy.550), calls=%async_computation | async-start | bytes 1048576 | tf_op jit(solution)/shard_map/all_to_all | solution.py:106
  32.6 28.4 %collective-permute-start.4 = (f32[4,2,1,256]{3,2,1,0:T(1,128)S(1)}, f32[4,2,1,256]{3,2,1,0:T(1,128)S(1)}, u32[]{:S(2)}, u32[]{:S(2)}) collective-permute-start(f32[4,2,1,256]{3,2,1,0:T(1,128)S(1)} %get-tuple-element.60), channel_id=1, source_target_pairs={{4,0},{8,4},{12,8},{16,12},{20,16},{24,20},{28,24},{32,28},{36,32}... | collective-permute-start | bytes 24584 | tf_op jit(solution)/shard_map/ppermute | solution.py:20
  33.9 27.1 %collective-permute-start.3 = (f32[4,2,1,256]{3,2,1,0:T(1,128)S(1)}, f32[4,2,1,256]{3,2,1,0:T(1,128)S(1)}, u32[]{:S(2)}, u32[]{:S(2)}) collective-permute-start(f32[4,2,1,256]{3,2,1,0:T(1,128)S(1)} %get-tuple-element.59), channel_id=1, source_target_pairs={{0,4},{4,8},{8,12},{12,16},{16,20},{20,24},{24,28},{28,32},{32,36}... | collective-permute-start | bytes 24584 | tf_op jit(solution)/shard_map/ppermute | solution.py:17
  37.9 13.5 %collective-permute-start.1 = (f32[2,1,256]{2,1,0:T(1,128)S(1)}, f32[2,1,256]{2,1,0:T(1,128)S(1)}, u32[]{:S(2)}, u32[]{:S(2)}) collective-permute-start(f32[2,1,256]{2,1,0:T(1,128)S(1)} %get-tuple-element.74), channel_id=1, source_target_pairs={{4,0},{8,4},{12,8},{16,12},{20,16},{24,20},{28,24},{32,28},{36,32}... | collective-permute-start | bytes 6152 | tf_op jit(solution)/shard_map/ppermute | solution.py:20
  40.4 6.3 %collective-permute-start.21 = (f32[1,1,128]{2,1,0:T(1,128)S(1)}, f32[1,1,128]{2,1,0:T(1,128)S(1)}, u32[]{:S(2)}, u32[]{:S(2)}) collective-permute-start(f32[1,1,128]{2,1,0:T(1,128)S(1)} %get-tuple-element.93), channel_id=1, source_target_pairs={{4,0},{8,4},{12,8},{16,12},{20,16},{24,20},{28,24},{32,28},{36,32}... | collective-permute-start | bytes 1544 | tf_op jit(solution)/shard_map/ppermute | solution.py:20
  41.7 8.3 %collective-permute-start.20 = (f32[1,1,128]{2,1,0:T(1,128)S(1)}, f32[1,1,128]{2,1,0:T(1,128)S(1)}, u32[]{:S(2)}, u32[]{:S(2)}) collective-permute-start(f32[1,1,128]{2,1,0:T(1,128)S(1)} %get-tuple-element.92), channel_id=1, source_target_pairs={{0,4},{4,8},{8,12},{12,16},{16,20},{20,24},{24,28},{28,32},{32,36}... | collective-permute-start | bytes 1544 | tf_op jit(solution)/shard_map/ppermute | solution.py:17
  46.7 8.7 %collective-permute-start = (f32[2,1,256]{2,1,0:T(1,128)S(1)}, f32[2,1,256]{2,1,0:T(1,128)S(1)}, u32[]{:S(2)}, u32[]{:S(2)}) collective-permute-start(f32[2,1,256]{2,1,0:T(1,128)S(1)} %get-tuple-element.73), channel_id=1, source_target_pairs={{0,4},{4,8},{8,12},{12,16},{16,20},{20,24},{24,28},{28,32},{32,36}... | collective-permute-start | bytes 6152 | tf_op jit(solution)/shard_map/ppermute | solution.py:17
  50.1 6.7 %collective-permute-start.22 = (f32[1,10,128]{2,1,0:T(8,128)S(1)}, f32[1,10,128]{2,1,0:T(8,128)S(1)}, u32[]{:S(2)}, u32[]{:S(2)}) collective-permute-start(f32[1,10,128]{2,1,0:T(8,128)S(1)} %pad_maximum_fusion.95), channel_id=1, source_target_pairs={{1,0},{2,1},{3,2},{5,4},{6,5},{7,6},{9,8},{10,9},{11,10},{13,12},{... | collective-permute-start | bytes 15368 | tf_op jit(solution)/shard_map/ppermute | solution.py:20
  51.4 9.3 %collective-permute-start.23 = (f32[1,10,128]{2,1,0:T(8,128)S(1)}, f32[1,10,128]{2,1,0:T(8,128)S(1)}, u32[]{:S(2)}, u32[]{:S(2)}) collective-permute-start(f32[1,10,128]{2,1,0:T(8,128)S(1)} %pad_maximum_fusion.95), channel_id=1, source_target_pairs={{0,1},{1,2},{2,3},{4,5},{5,6},{6,7},{8,9},{9,10},{10,11},{12,13},{... | collective-permute-start | bytes 15368 | tf_op jit(solution)/shard_map/ppermute | solution.py:17
  55.5 11.1 %collective-permute-start.2 = (f32[1,18,256]{2,1,0:T(8,128)S(1)}, f32[1,18,256]{2,1,0:T(8,128)S(1)}, u32[]{:S(2)}, u32[]{:S(2)}) collective-permute-start(f32[1,18,256]{2,1,0:T(8,128)S(1)} %get-tuple-element.69), channel_id=1, source_target_pairs={{1,0},{2,1},{3,2},{5,4},{6,5},{7,6},{9,8},{10,9},{11,10},{13,12},{... | collective-permute-start | bytes 55304 | tf_op jit(solution)/shard_map/ppermute | solution.py:20
  56.8 9.8 %collective-permute-start.6 = (f32[1,18,256]{2,1,0:T(8,128)S(1)}, f32[1,18,256]{2,1,0:T(8,128)S(1)}, u32[]{:S(2)}, u32[]{:S(2)}) collective-permute-start(f32[1,18,256]{2,1,0:T(8,128)S(1)} %get-tuple-element.68), channel_id=1, source_target_pairs={{0,1},{1,2},{2,3},{4,5},{5,6},{6,7},{8,9},{9,10},{10,11},{12,13},{... | collective-permute-start | bytes 55304 | tf_op jit(solution)/shard_map/ppermute | solution.py:17
  61.0 10.3 %copy-start.3 = (f32[1,4,2,16,256]{4,3,2,1,0:T(8,128)S(1)}, f32[1,4,2,16,256]{4,3,2,1,0:T(8,128)}, u32[]{:S(2)}) copy-start(f32[1,4,2,16,256]{4,3,2,1,0:T(8,128)} %param.12) | copy-start | bytes 393220
  61.0 10.3 %copy-start.1 = (f32[1,4,4,2,16,256]{5,4,3,2,1,0:T(8,128)S(1)}, f32[1,4,4,2,16,256]{5,4,3,2,1,0:T(8,128)}, u32[]{:S(2)}) copy-start(f32[1,4,4,2,16,256]{5,4,3,2,1,0:T(8,128)} %param.14) | copy-start | bytes 1572868
  61.1 9.7 %collective-permute-start.5 = (f32[4,1,18,256]{3,2,1,0:T(8,128)S(1)}, f32[4,1,18,256]{3,2,1,0:T(8,128)S(1)}, u32[]{:S(2)}, u32[]{:S(2)}) collective-permute-start(f32[4,1,18,256]{3,2,1,0:T(8,128)S(1)} %get-tuple-element.30), channel_id=1, source_target_pairs={{1,0},{2,1},{3,2},{5,4},{6,5},{7,6},{9,8},{10,9},{11,10},{13,12},{... | collective-permute-start | bytes 221192 | tf_op jit(solution)/shard_map/ppermute | solution.py:20
  62.5 8.3 %collective-permute-start.7 = (f32[4,1,18,256]{3,2,1,0:T(8,128)S(1)}, f32[4,1,18,256]{3,2,1,0:T(8,128)S(1)}, u32[]{:S(2)}, u32[]{:S(2)}) collective-permute-start(f32[4,1,18,256]{3,2,1,0:T(8,128)S(1)} %get-tuple-element.29), channel_id=1, source_target_pairs={{0,1},{1,2},{2,3},{4,5},{5,6},{6,7},{8,9},{9,10},{10,11},{12,13},{... | collective-permute-start | bytes 221192 | tf_op jit(solution)/shard_map/ppermute | solution.py:17
  85.8 35.4 %collective-permute-start.9 = (f32[4,2,1,256]{3,2,1,0:T(1,128)S(1)}, f32[4,2,1,256]{3,2,1,0:T(1,128)S(1)}, u32[]{:S(2)}, u32[]{:S(2)}) collective-permute-start(f32[4,2,1,256]{3,2,1,0:T(1,128)S(1)} %get-tuple-element.56), channel_id=1, source_target_pairs={{4,0},{8,4},{12,8},{16,12},{20,16},{24,20},{28,24},{32,28},{36,32}... | collective-permute-start | bytes 24584 | tf_op jit(solution)/shard_map/ppermute | solution.py:20
  87.1 34.1 %collective-permute-start.8 = (f32[4,2,1,256]{3,2,1,0:T(1,128)S(1)}, f32[4,2,1,256]{3,2,1,0:T(1,128)S(1)}, u32[]{:S(2)}, u32[]{:S(2)}) collective-permute-start(f32[4,2,1,256]{3,2,1,0:T(1,128)S(1)} %get-tuple-element.55), channel_id=1, source_target_pairs={{0,4},{4,8},{8,12},{12,16},{16,20},{20,24},{24,28},{28,32},{32,36}... | collective-permute-start | bytes 24584 | tf_op jit(solution)/shard_map/ppermute | solution.py:17
  92.8 63.4 %all-to-all-start.1 = ((f32[128,4,2,4]{3,2,1,0:T(2,128)}), f32[128,4,2,4]{3,2,1,0:T(2,128)S(1)}, u32[]{:S(2)}, u32[]{:S(2)}) async-start(f32[128,4,2,4]{3,2,1,0:T(2,128)} %copy.559), calls=%async_computation.1 | async-start | bytes 1048576 | tf_op jit(solution)/shard_map/all_to_all | solution.py:106
  121.3 38.2 %collective-permute-start.10 = (f32[4,1,18,256]{3,2,1,0:T(8,128)S(1)}, f32[4,1,18,256]{3,2,1,0:T(8,128)S(1)}, u32[]{:S(2)}, u32[]{:S(2)}) collective-permute-start(f32[4,1,18,256]{3,2,1,0:T(8,128)S(1)} %get-tuple-element.28), channel_id=1, source_target_pairs={{1,0},{2,1},{3,2},{5,4},{6,5},{7,6},{9,8},{10,9},{11,10},{13,12},{... | collective-permute-start | bytes 221192 | tf_op jit(solution)/shard_map/ppermute | solution.py:20
  122.6 36.9 %collective-permute-start.11 = (f32[4,1,18,256]{3,2,1,0:T(8,128)S(1)}, f32[4,1,18,256]{3,2,1,0:T(8,128)S(1)}, u32[]{:S(2)}, u32[]{:S(2)}) collective-permute-start(f32[4,1,18,256]{3,2,1,0:T(8,128)S(1)} %get-tuple-element.27), channel_id=1, source_target_pairs={{0,1},{1,2},{2,3},{4,5},{5,6},{6,7},{8,9},{9,10},{10,11},{12,13},{... | collective-permute-start | bytes 221192 | tf_op jit(solution)/shard_map/ppermute | solution.py:17
  174.5 14.9 %collective-permute-start.13 = (f32[4,2,1,256]{3,2,1,0:T(1,128)S(1)}, f32[4,2,1,256]{3,2,1,0:T(1,128)S(1)}, u32[]{:S(2)}, u32[]{:S(2)}) collective-permute-start(f32[4,2,1,256]{3,2,1,0:T(1,128)S(1)} %get-tuple-element.52), channel_id=1, source_target_pairs={{4,0},{8,4},{12,8},{16,12},{20,16},{24,20},{28,24},{32,28},{36,32}... | collective-permute-start | bytes 24584 | tf_op jit(solution)/shard_map/ppermute | solution.py:20
  175.8 13.6 %collective-permute-start.12 = (f32[4,2,1,256]{3,2,1,0:T(1,128)S(1)}, f32[4,2,1,256]{3,2,1,0:T(1,128)S(1)}, u32[]{:S(2)}, u32[]{:S(2)}) collective-permute-start(f32[4,2,1,256]{3,2,1,0:T(1,128)S(1)} %get-tuple-element.51), channel_id=1, source_target_pairs={{0,4},{4,8},{8,12},{12,16},{16,20},{20,24},{24,28},{28,32},{32,36}... | collective-permute-start | bytes 24584 | tf_op jit(solution)/shard_map/ppermute | solution.py:17
  181.1 43.4 %all-to-all-start.2 = ((f32[128,4,2,4]{3,2,1,0:T(2,128)}), f32[128,4,2,4]{3,2,1,0:T(2,128)S(1)}, u32[]{:S(2)}, u32[]{:S(2)}) async-start(f32[128,4,2,4]{3,2,1,0:T(2,128)} %copy.567), calls=%async_computation.2 | async-start | bytes 1048576 | tf_op jit(solution)/shard_map/all_to_all | solution.py:106
  189.5 38.2 %collective-permute-start.14 = (f32[4,1,18,256]{3,2,1,0:T(8,128)S(1)}, f32[4,1,18,256]{3,2,1,0:T(8,128)S(1)}, u32[]{:S(2)}, u32[]{:S(2)}) collective-permute-start(f32[4,1,18,256]{3,2,1,0:T(8,128)S(1)} %get-tuple-element.26), channel_id=1, source_target_pairs={{1,0},{2,1},{3,2},{5,4},{6,5},{7,6},{9,8},{10,9},{11,10},{13,12},{... | collective-permute-start | bytes 221192 | tf_op jit(solution)/shard_map/ppermute | solution.py:20
  190.8 36.9 %collective-permute-start.15 = (f32[4,1,18,256]{3,2,1,0:T(8,128)S(1)}, f32[4,1,18,256]{3,2,1,0:T(8,128)S(1)}, u32[]{:S(2)}, u32[]{:S(2)}) collective-permute-start(f32[4,1,18,256]{3,2,1,0:T(8,128)S(1)} %get-tuple-element.25), channel_id=1, source_target_pairs={{0,1},{1,2},{2,3},{4,5},{5,6},{6,7},{8,9},{9,10},{10,11},{12,13},{... | collective-permute-start | bytes 221192 | tf_op jit(solution)/shard_map/ppermute | solution.py:17
  242.8 15.2 %collective-permute-start.17 = (f32[4,2,1,256]{3,2,1,0:T(1,128)S(1)}, f32[4,2,1,256]{3,2,1,0:T(1,128)S(1)}, u32[]{:S(2)}, u32[]{:S(2)}) collective-permute-start(f32[4,2,1,256]{3,2,1,0:T(1,128)S(1)} %get-tuple-element.48), channel_id=1, source_target_pairs={{4,0},{8,4},{12,8},{16,12},{20,16},{24,20},{28,24},{32,28},{36,32}... | collective-permute-start | bytes 24584 | tf_op jit(solution)/shard_map/ppermute | solution.py:20
  244.1 13.9 %collective-permute-start.16 = (f32[4,2,1,256]{3,2,1,0:T(1,128)S(1)}, f32[4,2,1,256]{3,2,1,0:T(1,128)S(1)}, u32[]{:S(2)}, u32[]{:S(2)}) collective-permute-start(f32[4,2,1,256]{3,2,1,0:T(1,128)S(1)} %get-tuple-element.47), channel_id=1, source_target_pairs={{0,4},{4,8},{8,12},{12,16},{16,20},{20,24},{24,28},{28,32},{32,36}... | collective-permute-start | bytes 24584 | tf_op jit(solution)/shard_map/ppermute | solution.py:17
  249.3 43.6 %all-to-all-start.3 = ((f32[128,4,2,4]{3,2,1,0:T(2,128)}), f32[128,4,2,4]{3,2,1,0:T(2,128)S(1)}, u32[]{:S(2)}, u32[]{:S(2)}) async-start(f32[128,4,2,4]{3,2,1,0:T(2,128)} %copy.575), calls=%async_computation.3 | async-start | bytes 1048576 | tf_op jit(solution)/shard_map/all_to_all | solution.py:106
  258.0 38.2 %collective-permute-start.18 = (f32[4,1,18,256]{3,2,1,0:T(8,128)S(1)}, f32[4,1,18,256]{3,2,1,0:T(8,128)S(1)}, u32[]{:S(2)}, u32[]{:S(2)}) collective-permute-start(f32[4,1,18,256]{3,2,1,0:T(8,128)S(1)} %get-tuple-element.24), channel_id=1, source_target_pairs={{1,0},{2,1},{3,2},{5,4},{6,5},{7,6},{9,8},{10,9},{11,10},{13,12},{... | collective-permute-start | bytes 221192 | tf_op jit(solution)/shard_map/ppermute | solution.py:20
  259.3 36.9 %collective-permute-start.19 = (f32[4,1,18,256]{3,2,1,0:T(8,128)S(1)}, f32[4,1,18,256]{3,2,1,0:T(8,128)S(1)}, u32[]{:S(2)}, u32[]{:S(2)}) collective-permute-start(f32[4,1,18,256]{3,2,1,0:T(8,128)S(1)} %get-tuple-element.23), channel_id=1, source_target_pairs={{0,1},{1,2},{2,3},{4,5},{5,6},{6,7},{8,9},{9,10},{10,11},{12,13},{... | collective-permute-start | bytes 221192 | tf_op jit(solution)/shard_map/ppermute | solution.py:17
  299.4 6.0 %collective-permute-start.25 = (f32[4,1,1,128]{3,2,0,1:T(1,128)S(1)}, f32[4,1,1,128]{3,2,0,1:T(1,128)S(1)}, u32[]{:S(2)}, u32[]{:S(2)}) collective-permute-start(f32[4,1,1,128]{3,2,0,1:T(1,128)S(1)} %get-tuple-element.82), channel_id=1, source_target_pairs={{4,0},{8,4},{12,8},{16,12},{20,16},{24,20},{28,24},{32,28},{36,32}... | collective-permute-start | bytes 6152 | tf_op jit(solution)/shard_map/ppermute | solution.py:20
  300.7 4.7 %collective-permute-start.24 = (f32[4,1,1,128]{3,2,0,1:T(1,128)S(1)}, f32[4,1,1,128]{3,2,0,1:T(1,128)S(1)}, u32[]{:S(2)}, u32[]{:S(2)}) collective-permute-start(f32[4,1,1,128]{3,2,0,1:T(1,128)S(1)} %get-tuple-element.81), channel_id=1, source_target_pairs={{0,4},{4,8},{8,12},{12,16},{16,20},{20,24},{24,28},{28,32},{32,36}... | collective-permute-start | bytes 6152 | tf_op jit(solution)/shard_map/ppermute | solution.py:17
  305.4 5.3 %collective-permute-start.26 = (f32[4,1,10,128]{3,0,2,1:T(4,128)S(1)}, f32[4,1,10,128]{3,0,2,1:T(4,128)S(1)}, u32[]{:S(2)}, u32[]{:S(2)}) collective-permute-start(f32[4,1,10,128]{3,0,2,1:T(4,128)S(1)} %pad_maximum_fusion.94), channel_id=1, source_target_pairs={{1,0},{2,1},{3,2},{5,4},{6,5},{7,6},{9,8},{10,9},{11,10},{13,12},{... | collective-permute-start | bytes 61448 | tf_op jit(solution)/shard_map/ppermute | solution.py:20
  306.7 4.9 %collective-permute-start.27 = (f32[4,1,10,128]{3,0,2,1:T(4,128)S(1)}, f32[4,1,10,128]{3,0,2,1:T(4,128)S(1)}, u32[]{:S(2)}, u32[]{:S(2)}) collective-permute-start(f32[4,1,10,128]{3,0,2,1:T(4,128)S(1)} %pad_maximum_fusion.94), channel_id=1, source_target_pairs={{0,1},{1,2},{2,3},{4,5},{5,6},{6,7},{8,9},{9,10},{10,11},{12,13},{... | collective-permute-start | bytes 61448 | tf_op jit(solution)/shard_map/ppermute | solution.py:17
where the time goes:
time: 317 us; the launch traced here: 312 us
  starting transfers between devices  141 us (44%)
  waiting for transfers between devices  90.5 us (29%)
  local copies, waits for them, and re-layouts  50 us (16%)
  other arithmetic  29.4 us (9%)
    all_to_all x4, waiting for transfers between devices, rim_ghosts(): lax.all_to_all(doubled, ('patch', 'lat'), split_axis=0, concat_axis=0, ti...  89.6 us
    all_to_all x4, starting transfers between devices, rim_ghosts(): lax.all_to_all(doubled, ('patch', 'lat'), split_axis=0, concat_axis=0, ti...  66.2 us
    ppermute x14, starting transfers between devices, padded_2(): lax.ppermute(lax.slice_in_dim(block, block.shape[dim] - width, None, axis...  56.3 us
    add x7, other arithmetic, shards(): iterate = iterate + OMEGA * jnp.sum(inverse * residual[None], axis=1)  20.6 us
    ppermute x14, starting transfers between devices, padded_2(): lax.ppermute(lax.slice_in_dim(block, 0, width, axis=dim), axis, backward)  18.2 us
    gather x4, local copies, waits for them, and re-layouts, rim_ghosts(): jnp.take(flat, cells.reshape(-1), axis=2)  12.7 us
    mul x3, local copies, waits for them, and re-layouts, shards(): iterate = iterate + OMEGA * jnp.sum(inverse * residual[None], axis=1)  9.5 us
  transfers between devices with their start and end apart: 32, of which 5 were waited for; matrix products, arithmetic and copies ran while one was open for 6% of the time, Pallas kernels for 0%

commit v1 on v0

v1 whole, which is shorter than its diff:
```python
import functools

import jax
import jax.numpy as jnp
from jax import lax
from jax.experimental import pallas as pl
from jax.experimental.pallas import tpu as pltpu
from jax.sharding import PartitionSpec as P

SWEEPS = 3
OMEGA = 0.8
WIN = 32
CAP = 4
RIM, RAD, PHI, ETA_RAD, COARSE_RAD, ETA_PHI, FIRST_RAD, FIRST_PHI = 0, 4, 12, 20, 22, 24, 26, 28
F32 = jnp.float32


def exact_dot(values, zero_one):
    high = values.astype(jnp.bfloat16)
    rest = values - high.astype(F32)
    middle = rest.astype(jnp.bfloat16)
    low = (rest - middle.astype(F32)).astype(jnp.bfloat16)
    dot = functools.partial(jnp.dot, preferred_element_type=F32)
    return dot(high, zero_one) + (dot(middle, zero_one) + dot(low, zero_one))


def kernel(
    strips, layers,
    iterate_hbm, forcing_hbm, eta_hbm, inverse_hbm, cells_hbm, slots_hbm, weights_hbm,
    iterate_out, coarse_out,
    cur, frc, eta, vin, cel, slt, wgt,
    onehot, pick, pick_edge, weigh, diag, w_phi, w_lat, w_rad, inv_eta, gain, edge_w, edge_ie,
    rim_send, rim_recv, rad_recv, phi_send, phi_recv,
    eta_rad, eta_phi_send, eta_phi, ceta, ceta_rad, cdia, cfaces,
    first, first_rad, first_phi_send, first_phi, fold,
    local_sem, send_sem, recv_sem,
):
    patch, lat, rad = lax.axis_index("patch"), lax.axis_index("lat"), lax.axis_index("rad")
    _, _, width, na = frc.shape
    half = na // 2
    below = (patch, lat, lax.rem(rad + layers - 1, layers))
    above = (patch, lat, lax.rem(rad + 1, layers))
    left = (patch, lax.rem(lat + strips - 1, strips), rad)
    right = (patch, lax.rem(lat + 1, strips), rad)
    has_below, has_above = rad > 0, rad < layers - 1
    has_left, has_right = lat > 0, lat < strips - 1

    def across(offset):
        return (1 - patch, lax.rem(lat + offset + strips, strips), rad)

    loads = [
        pltpu.make_async_copy(iterate_hbm, cur.at[0], local_sem.at[0]),
        pltpu.make_async_copy(cells_hbm, cel.at[pl.ds(0, strips)], local_sem.at[1]),
        pltpu.make_async_copy(cells_hbm, cel.at[pl.ds(strips, strips)], local_sem.at[2]),
        pltpu.make_async_copy(eta_hbm, eta, local_sem.at[3]),
        pltpu.make_async_copy(slots_hbm, slt, local_sem.at[4]),
        pltpu.make_async_copy(weights_hbm, wgt, local_sem.at[5]),
        pltpu.make_async_copy(forcing_hbm, frc, local_sem.at[6]),
    ]
    for i in range(4):
        loads.append(
            pltpu.make_async_copy(
                inverse_hbm.at[i, pl.ds(i, 4 - i)], vin.at[i, pl.ds(i, 4 - i)], local_sem.at[7 + i]
            )
        )
    for load in loads:
        load.start()

    barrier = pltpu.get_barrier_semaphore()

    def greet(device):
        pl.semaphore_signal(barrier, inc=1, device_id=device, device_id_type=pl.DeviceIdType.MESH)

    for offset in sorted(range(-WIN // 2, WIN // 2), key=lambda o: -abs(o)):
        greet(across(offset))
    for device in (below, above, left, right):
        greet(device)

    def remote(src, dst, sem, device):
        return pltpu.make_async_remote_copy(
            src_ref=src, dst_ref=dst, send_sem=send_sem.at[sem], recv_sem=recv_sem.at[sem],
            device_id=device, device_id_type=pl.DeviceIdType.MESH,
        )

    def rad_copies(k):
        return [
            remote(cur.at[k, :, 1], rad_recv.at[k, 0], RAD + 2 * k, above),
            remote(cur.at[k, :, 0], rad_recv.at[k, 1], RAD + 2 * k + 1, below),
        ]

    def phi_copies(k):
        return [
            remote(phi_send.at[k, 0], phi_recv.at[k, 0], PHI + 2 * k, right),
            remote(phi_send.at[k, 1], phi_recv.at[k, 1], PHI + 2 * k + 1, left),
        ]

    def rim_start(k):
        for slot in sorted(range(WIN), key=lambda s: -abs(s - WIN // 2 + 1)):
            remote(
                rim_send.at[k, pl.ds(slot, 1)], rim_recv.at[k, pl.ds(WIN - 1 - slot, 1)], RIM + k,
                across(slot - WIN // 2 + 1),
            ).start()

    def rim_all(k, sem):
        return pltpu.make_async_copy(rim_recv.at[k], rim_recv.at[k], sem.at[RIM + k])

    eta_copies = [
        remote(eta.at[1], eta_rad.at[0], ETA_RAD, above),
        remote(eta.at[0], eta_rad.at[1], ETA_RAD + 1, below),
        remote(ceta, ceta_rad.at[0], COARSE_RAD, above),
        remote(ceta, ceta_rad.at[1], COARSE_RAD + 1, below),
        remote(eta_phi_send.at[0], eta_phi.at[0], ETA_PHI, right),
        remote(eta_phi_send.at[1], eta_phi.at[1], ETA_PHI + 1, left),
    ]
    first_copies = [
        remote(first, first_rad.at[0], FIRST_RAD, above),
        remote(first, first_rad.at[1], FIRST_RAD + 1, below),
        remote(first_phi_send.at[0], first_phi.at[0], FIRST_PHI, right),
        remote(first_phi_send.at[1], first_phi.at[1], FIRST_PHI + 1, left),
    ]

    def iota(shape, dim):
        return lax.broadcasted_iota(jnp.int32, shape, dim)

    lane, row = iota((width, na), 1), iota((width, na), 0)
    tile_lane = iota((width, half), 1)
    slot_lane = iota((8, WIN * CAP), 1)

    def shift(x, dim, up, fill):
        count = x.shape[dim]
        at = iota(x.shape, dim)
        rolled = pltpu.roll(x, count - 1 if up else 1, dim)
        return jnp.where(at == (count - 1 if up else 0), fill, rolled)

    def put_rim(k, packed):
        tall = jnp.concatenate([jnp.where(slot_lane // WIN == s, packed, 0.0) for s in range(CAP)], axis=0)
        turned = tall.T
        rows = turned[0:WIN]
        for s in range(1, CAP):
            rows = rows + turned[s * WIN : (s + 1) * WIN]
        rim_send[k, :, 0 : 8 * CAP] = rows

    def pack(field):
        found = exact_dot(field, onehot[...]).reshape(8, width, WIN * CAP)
        return jnp.sum(found * pick[...][None], axis=1)

    def put_edges(k):
        for c in range(4):
            for r in range(2):
                phi_send[k, 0, 2 * c + r, :] = cur[k, c, r, width - 1, :]
                phi_send[k, 1, 2 * c + r, :] = cur[k, c, r, 0, :]

    pairs = (iota((na, half), 0) // 2 == iota((na, half), 1)).astype(F32).astype(jnp.bfloat16)

    def fold_rows(count):
        return fold[pl.ds(0, count, stride=2), :] + fold[pl.ds(1, count, stride=2), :]

    rim_send[...] = jnp.zeros_like(rim_send)
    eta_phi_send[...] = jnp.zeros_like(eta_phi_send)
    loads[1].wait()
    loads[2].wait()
    mine = cel[pl.ds(lax.rem(lat + strips - WIN // 2 + 1, strips), WIN), :].astype(F32)
    lanes = iota((WIN, WIN * CAP), 1)
    spread = jnp.zeros((WIN, WIN * CAP), F32)
    for s in range(CAP):
        spread = jnp.where(lanes // WIN == s, mine[:, s : s + 1], spread)
    spread = jnp.where(lanes % WIN == iota((WIN, WIN * CAP), 0), spread, 0.0)
    cell = jnp.sum(spread, axis=0, keepdims=True).astype(jnp.int32)
    cell_lat, cell_lon = cell % na, cell // na
    onehot[...] = (iota((na, WIN * CAP), 0) == cell_lat).astype(F32).astype(jnp.bfloat16)
    in_lon = (iota((width, WIN * CAP), 0) == cell_lon).astype(F32)
    pick[...] = in_lon
    pick_edge[0] = jnp.where(cell_lat == 0, in_lon, 0.0)
    pick_edge[1] = jnp.where(cell_lat == na - 1, in_lon, 0.0)
    loads[0].wait()
    put_rim(0, pack(cur[0].reshape(8 * width, na)))
    put_edges(0)

    loads[3].wait()
    fold[0:width, :] = exact_dot(eta[0] + eta[1], pairs)
    coarse_eta = 0.125 * fold_rows(width // 2)
    ceta[...] = coarse_eta
    for r in range(2):
        eta_phi_send[0, r, :] = eta[r, width - 1, :]
        eta_phi_send[1, r, :] = eta[r, 0, :]
    eta_phi_send[0, 2, 0:half] = ceta[width // 2 - 1, :]
    eta_phi_send[1, 2, 0:half] = ceta[0, :]

    pl.semaphore_wait(barrier, WIN + 4)
    rim_start(0)
    for copy in rad_copies(0) + phi_copies(0) + eta_copies:
        copy.start()

    for load in loads[4:]:
        load.wait()
    lanes = iota((2 * width, WIN * CAP), 1)
    slot_here = lax.rem(lanes % WIN + lat + strips - WIN // 2, strips) * CAP + lanes // WIN
    total = jnp.zeros((2 * width, WIN * CAP), F32)
    for s in range(4):
        total = total + jnp.where(slt[:, s : s + 1] == slot_here, wgt[:, s : s + 1], 0.0)
    weigh[...] = total

    for copy in eta_copies:
        copy.wait_recv()
    eta_below = jnp.where(has_below, eta_rad[0], 0.0)
    eta_above = jnp.where(has_above, eta_rad[1], 0.0)
    w_rad[0] = 0.5 * (eta[0] + eta_below)
    w_rad[1] = 0.5 * (eta[0] + eta[1])
    w_rad[2] = 0.5 * (eta[1] + eta_above)
    for r in range(2):
        own = eta[r]
        low_row = jnp.where(has_left, eta_phi[0, r : r + 1, :], 0.0)
        high_row = jnp.where(has_right, eta_phi[1, r : r + 1, :], 0.0)
        phi_low = 0.5 * (own + shift(own, 0, False, low_row))
        phi_high = 0.5 * (own + shift(own, 0, True, high_row))
        lat_low = 0.5 * (own + shift(own, 1, False, own))
        lat_high = 0.5 * (own + shift(own, 1, True, own))
        inverse_eta = 1.0 / own
        w_phi[0, r], w_phi[1, r] = phi_low, phi_high
        w_lat[0, r], w_lat[1, r] = lat_low, lat_high
        inv_eta[r] = inverse_eta
        diag[r] = w_rad[r] + w_rad[r + 1] + (phi_low + phi_high) + (lat_low + lat_high)
        for e in range(2):
            at = 0 if e == 0 else na - 1

            def column(x, at=at):
                return jnp.broadcast_to(x[:, at : at + 1], (width, half))

            sign = 0.5 if e == 0 else -0.5
            w = column(lat_low if e == 0 else lat_high)
            ie = column(inverse_eta)
            edge_w[e, r], edge_ie[e, r] = w, ie
            for i in range(4):
                v = [OMEGA * column(vin[min(i, j), max(i, j), r]) for j in range(4)]
                gain[e, i, 0, r] = v[0] * w
                gain[e, i, 1, r] = v[1] * w
                gain[e, i, 2, r] = v[2] * w - sign * v[3]
                gain[e, i, 3, r] = v[3] * ie + sign * v[2]

    own = ceta[...]
    c_below = jnp.where(has_below, ceta_rad[0], 0.0)
    c_above = jnp.where(has_above, ceta_rad[1], 0.0)
    c_left = jnp.where(has_left, eta_phi[0, 2:3, 0:half], 0.0)
    c_right = jnp.where(has_right, eta_phi[1, 2:3, 0:half], 0.0)
    faces = [
        0.5 * (own + c_below), 0.5 * (own + c_above),
        0.5 * (own + shift(own, 0, False, c_left)), 0.5 * (own + shift(own, 0, True, c_right)),
        0.5 * (own + shift(own, 1, False, own)), 0.5 * (own + shift(own, 1, True, own)),
    ]
    for n, face in enumerate(faces):
        cfaces[n] = face
    faces_sum = (faces[0] + faces[1]) + (faces[2] + faces[3]) + (faces[4] + faces[5])
    cdia[0] = faces_sum
    cdia[1] = OMEGA / (0.25 * faces_sum)
    cdia[2] = OMEGA / (0.25 * (6.0 / own))
    cdia[3] = 1.0 / own

    def residual(k):
        result = [[None, None] for _ in range(4)]
        sums = [None, None]
        flows = [None, None]
        for r in range(2):
            v = [cur[k, c, r] for c in range(4)]
            other = [cur[k, c, 1 - r] for c in range(4)]
            lo = [shift(v[c], 1, False, 0.0) for c in range(4)]
            hi = [shift(v[c], 1, True, 0.0) for c in range(4)]
            for c in range(3):
                result[c][r] = (
                    frc[c, r] - diag[r] * v[c] + w_rad[1] * other[c] + w_lat[0, r] * lo[c] + w_lat[1, r] * hi[c]
                )
            result[2][r] = result[2][r] + 0.5 * (lo[3] - hi[3])
            sums[r] = other[3] + lo[3] + hi[3] - 6.0 * v[3]
            flows[r] = hi[2] - lo[2]
            if r == 0:
                result[0][r] = result[0][r] - 0.5 * other[3]
                flows[r] = flows[r] + other[0]
            else:
                result[0][r] = result[0][r] + 0.5 * other[3]
                flows[r] = flows[r] - other[0]
        for copy in phi_copies(k):
            copy.wait_recv()
        for r in range(2):
            lo, hi = [], []
            for c in range(4):
                v = cur[k, c, r]
                n = 2 * c + r
                lo.append(shift(v, 0, False, jnp.where(has_left, phi_recv[k, 0, n : n + 1, :], 0.0)))
                hi.append(shift(v, 0, True, jnp.where(has_right, phi_recv[k, 1, n : n + 1, :], 0.0)))
            for c in range(3):
                result[c][r] = result[c][r] + w_phi[0, r] * lo[c] + w_phi[1, r] * hi[c]
            result[1][r] = result[1][r] + 0.5 * (lo[3] - hi[3])
            sums[r] = sums[r] + lo[3] + hi[3]
            flows[r] = flows[r] + (hi[1] - lo[1])
        for copy in rad_copies(k):
            copy.wait_recv()
        for r in range(2):
            has, sign, w = (has_below, 0.5, w_rad[0]) if r == 0 else (has_above, -0.5, w_rad[2])
            n = [jnp.where(has, rad_recv[k, r, c], 0.0) for c in range(4)]
            for c in range(3):
                result[c][r] = result[c][r] + w * n[c]
            result[0][r] = result[0][r] + sign * n[3]
            flow = flows[r] - n[0] if r == 0 else flows[r] + n[0]
            result[3][r] = frc[3, r] + inv_eta[r] * (sums[r] + n[3]) + 0.5 * flow
        return result

    def ghosts(k):
        rim_all(k, recv_sem).wait()
        turned = rim_recv[k].T
        by_slot = jnp.concatenate([turned[8 * s : 8 * s + 8] for s in range(CAP)], axis=1)
        return jnp.sum(by_slot[:, None, :] * weigh[...][None], axis=-1, keepdims=True)

    def sent(k):
        for copy in rad_copies(k) + phi_copies(k):
            copy.wait_send()
        rim_all(k, send_sem).wait()

    def sweep(k, carry):
        res = residual(k)
        scaled = [[OMEGA * res[j][r] for r in range(2)] for j in range(4)]
        for i in range(4):
            for r in range(2):
                gained = cur[k, i, r]
                for j in range(4):
                    gained = gained + vin[min(i, j), max(i, j), r] * scaled[j][r]
                cur[k + 1, i, r] = gained
        packed = pack(cur[k + 1].reshape(8 * width, na))
        sent(k)
        ghost = ghosts(k)
        deltas = []
        for e in range(2):
            delta = []
            for i in range(4):
                for r in range(2):
                    value = jnp.zeros((width, half), F32)
                    for j in range(4):
                        value = value + gain[e, i, j, r] * ghost[2 * j + r, e * width : (e + 1) * width, :]
                    delta.append(value)
            deltas.append(delta)
        at_edge = jnp.stack(
            [deltas[0][n] * pick_edge[0] + deltas[1][n] * pick_edge[1] for n in range(8)], axis=0
        )
        put_rim(k + 1, packed + jnp.sum(at_edge, axis=1))
        rim_start(k + 1)
        for i in range(4):
            for r in range(2):
                n = 2 * i + r
                cur[k + 1, i, r, :, 0:half] += jnp.where(tile_lane == 0, deltas[0][n], 0.0)
                cur[k + 1, i, r, :, half:na] += jnp.where(tile_lane == half - 1, deltas[1][n], 0.0)
        put_edges(k + 1)
        for copy in rad_copies(k + 1) + phi_copies(k + 1):
            copy.start()
        return carry

    lax.fori_loop(0, SWEEPS, sweep, 0)
    store = pltpu.make_async_copy(cur.at[SWEEPS], iterate_out, local_sem.at[0])
    store.start()
    for copy in eta_copies:
        copy.wait_send()

    res = residual(SWEEPS)
    summed = jnp.concatenate([res[c][0] + res[c][1] for c in range(4)], axis=0)
    fold[...] = exact_dot(summed, pairs)
    base = fold_rows(4 * (width // 2))
    sent(SWEEPS)
    ghost = ghosts(SWEEPS)
    tops = []
    for e in range(2):
        sign = 0.5 if e == 0 else -0.5
        terms = [jnp.zeros((width, half), F32) for _ in range(4)]
        for r in range(2):
            g = [ghost[2 * j + r, e * width : (e + 1) * width, :] for j in range(4)]
            for c in range(3):
                terms[c] = terms[c] + edge_w[e, r] * g[c]
            terms[2] = terms[2] + sign * g[3]
            terms[3] = terms[3] + (edge_ie[e, r] * g[3] - sign * g[2])
        fold[...] = jnp.concatenate(terms, axis=0)
        tops.append(fold_rows(4 * (width // 2)))
    lanes = iota(base.shape, 1)
    coarse = base + jnp.where(lanes == 0, tops[0], 0.0) + jnp.where(lanes == half - 1, tops[1], 0.0)
    coarse = (0.125 * coarse).reshape(4, width // 2, half)
    for c in range(4):
        first[c] = coarse[c] * cdia[1 if c < 3 else 2]
    for c in range(4):
        first_phi_send[0, c, :] = first[c, width // 2 - 1, :]
        first_phi_send[1, c, :] = first[c, 0, :]
    for copy in first_copies:
        copy.start()
    one = [first[c] for c in range(4)]
    lat_lo = [shift(one[c], 1, False, 0.0) for c in range(4)]
    lat_hi = [shift(one[c], 1, True, 0.0) for c in range(4)]
    for copy in first_copies:
        copy.wait_recv()
    low, high = [], []
    low.append([jnp.where(has_below, first_rad[0, c], 0.0) for c in range(4)])
    high.append([jnp.where(has_above, first_rad[1, c], 0.0) for c in range(4)])
    low.append([shift(one[c], 0, False, jnp.where(has_left, first_phi[0, c : c + 1, :], 0.0)) for c in range(4)])
    high.append([shift(one[c], 0, True, jnp.where(has_right, first_phi[1, c : c + 1, :], 0.0)) for c in range(4)])
    low.append(lat_lo)
    high.append(lat_hi)
    pressure = 6.0 * one[3]
    flow = jnp.zeros_like(pressure)
    for d in range(3):
        pressure = pressure - low[d][3] - high[d][3]
        flow = flow + (high[d][d] - low[d][d])
    for c in range(3):
        friction = cdia[0] * one[c]
        for d in range(3):
            friction = friction - cfaces[2 * d] * low[d][c] - cfaces[2 * d + 1] * high[d][c]
        applied = 0.25 * friction + 0.25 * (high[c][3] - low[c][3])
        coarse_out[c] = one[c] + cdia[1] * (coarse[c] - applied)
    applied = 0.25 * pressure * cdia[3] - 0.25 * flow
    coarse_out[3] = one[3] + cdia[2] * (coarse[3] - applied)
    for copy in first_copies:
        copy.wait_send()
    store.wait()


def shards(strips, layers, iterate_in, forcing, viscosity, vanka_inverse, pack_cells, take_slot, take_weight):
    _, comps, radial, width, na = iterate_in.shape
    half = na // 2
    field = (comps, radial, width, na)
    slots = WIN * CAP
    rounds = SWEEPS + 1

    def vmem(*shape, dtype=F32):
        return pltpu.VMEM(shape, dtype)

    scratch = [
        vmem(rounds, *field), vmem(*field), vmem(radial, width, na), vmem(4, *field),
        vmem(2 * strips, CAP, dtype=jnp.int32), vmem(2 * width, 4, dtype=jnp.int32), vmem(2 * width, 4),
        vmem(na, slots, dtype=jnp.bfloat16), vmem(width, slots), vmem(2, width, slots), vmem(2 * width, slots),
        vmem(radial, width, na), vmem(2, radial, width, na), vmem(2, radial, width, na), vmem(3, width, na),
        vmem(radial, width, na), vmem(2, 4, 4, radial, width, half), vmem(2, radial, width, half),
        vmem(2, radial, width, half),
        vmem(rounds, WIN, 128), vmem(rounds, WIN, 128), vmem(rounds, 2, comps, width, na),
        vmem(rounds, 2, 2 * comps, na), vmem(rounds, 2, 2 * comps, na),
        vmem(2, width, na), vmem(2, 8, na), vmem(2, 8, na), vmem(width // 2, half), vmem(2, width // 2, half),
        vmem(4, width // 2, half), vmem(6, width // 2, half),
        vmem(comps, width // 2, half), vmem(2, comps, width // 2, half), vmem(2, comps, half), vmem(2, comps, half),
        vmem(comps * width, half),
        pltpu.SemaphoreType.DMA((11,)), pltpu.SemaphoreType.DMA((30,)), pltpu.SemaphoreType.DMA((30,)),
    ]
    anywhere = pl.BlockSpec(memory_space=pl.ANY)
    iterate, coarse = pl.pallas_call(
        functools.partial(kernel, strips, layers),
        out_shape=(
            jax.ShapeDtypeStruct(field, F32),
            jax.ShapeDtypeStruct((comps, width // 2, half), F32),
        ),
        in_specs=[anywhere] * 7,
        out_specs=(anywhere, pl.BlockSpec(memory_space=pltpu.VMEM)),
        scratch_shapes=scratch,
        compiler_params=pltpu.CompilerParams(
            collective_id=0, has_side_effects=True, vmem_limit_bytes=32 * 1024 * 1024
        ),
        cost_estimate=pl.CostEstimate(flops=8_000_000, bytes_accessed=1_000_000, transcendentals=0),
    )(
        iterate_in[0], forcing[0], viscosity[0], vanka_inverse[0], pack_cells[0, 0], take_slot[0, 0], take_weight[0, 0],
    )
    return iterate[None], coarse[None, :, None]


def solution(mesh):
    in_specs = (
        P("patch", None, "rad", "lat", None),
        P("patch", None, "rad", "lat", None),
        P("patch", "rad", "lat", None),
        P("patch", None, None, "rad", "lat", None),
        P("patch", "lat", None, None),
        P("patch", "lat", None, None),
        P("patch", "lat", None, None),
    )
    out_specs = (P("patch", None, "rad", "lat", None), P("patch", None, "rad", "lat", None))
    part = functools.partial(shards, mesh.shape["lat"], mesh.shape["rad"])
    return jax.shard_map(part, mesh=mesh, in_specs=in_specs, out_specs=out_specs, check_vma=False)
```

time: 317 us -> 50.7 us (0.16); the launches traced: 312 us -> 50.4 us
  starting transfers between devices: 141 us -> 0 us
  waiting for transfers between devices: 90.5 us -> 0 us
  local copies, waits for them, and re-layouts: 50 us -> 5.64 us
  Pallas kernels: 0 us -> 44.1 us
  other arithmetic: 29.4 us -> 0 us
    all_to_all x4 -> x0, waiting for transfers between devices: 89.6 us -> none  [rim_ghosts(): lax.all_to_all(doubled, ('patch', 'lat'), split_axis=0, concat_axis=0, ti...]
    ppermute x28 -> x0, starting transfers between devices: 74.5 us -> none  [the longest x14 56.3 us: padded_2(): lax.ppermute(lax.slice_in_dim(block, block.shape[dim] - width, None, axis...]
    all_to_all x4 -> x0, starting transfers between devices: 66.2 us -> none  [rim_ghosts(): lax.all_to_all(doubled, ('patch', 'lat'), split_axis=0, concat_axis=0, ti...]
    pallas_call x0 -> x1, Pallas kernels: none -> 44.1 us  [shards(): pl.pallas_call(functools.partial(kernel, strips, layers), out_shape=(jax....]
    add x9 -> x0, other arithmetic: 21.3 us -> none  [the longest x7 20.6 us: shards(): iterate = iterate + OMEGA * jnp.sum(inverse * residual[None], axis=1)]
    gather x8 -> x0, local copies, waits for them, and re-layouts: 15.7 us -> none  [the longest x4 12.7 us: rim_ghosts(): jnp.take(flat, cells.reshape(-1), axis=2)]
    reshape x12 -> x0, local copies, waits for them, and re-layouts: 9.87 us -> none  [the longest x4 4.08 us: rim_ghosts(): jnp.take(flat, cells.reshape(-1), axis=2)]
    mul x4 -> x0, local copies, waits for them, and re-layouts: 9.59 us -> none  [the longest x3 9.5 us: shards(): iterate = iterate + OMEGA * jnp.sum(inverse * residual[None], axis=1)]
  transfers between devices with their start and end apart: 32 -> 0, of which waited for: 5 -> 0; matrix products, arithmetic and copies ran while one was open for 6% -> 0% of each run, Pallas kernels for 0% -> 0%
where the time goes in v1:
time: 50.7 us; the launch traced here: 50.4 us
  Pallas kernels  44.1 us (87%)
  local copies, waits for them, and re-layouts  5.64 us (11%)
  between operations  0.67 us (1%)
    pallas_call x1, Pallas kernels, shards(): pl.pallas_call(functools.partial(kernel, strips, layers), out_shape=(jax....  44.1 us
    unnamed x17, local copies, waits for them, and re-layouts  5.47 us

profile of v1, /device:TPU:1, one launch (start us, length us, event | category | flops | bytes accessed | tf_op | source)
XLA Modules:
  0.0 50.4 jit_solution(5169801759325159195)
XLA Ops:
  0.6 0.0 copy-start.4
  0.6 0.0 copy-start.5
  0.7 0.7 %copy-done.4 = s32[1,1,32,4]{2,3,1,0:T(4,128)S(1)} copy-done((s32[1,1,32,4]{2,3,1,0:T(4,128)S(1)}, s32[1,1,32,4]{2,3,1,0:T(4,128)}, u32[]{:S(2)}) %copy-start.4) | copy-done | bytes 536
  1.3 0.0 copy-start.3
  1.3 0.1 copy.10.slots_hbm
  1.4 0.0 copy-done.5
  1.4 0.0 copy-start.6
  1.4 0.1 copy.11.weights_hbm
  1.5 0.6 %copy-done.6 = s32[1,1,64,4]{2,3,1,0:T(4,128)S(1)} copy-done((s32[1,1,64,4]{2,3,1,0:T(4,128)S(1)}, s32[1,1,64,4]{2,3,1,0:T(4,128)}, u32[]{:S(2)}) %copy-start.6) | copy-done | bytes 1048
  2.1 0.1 copy.9
  2.2 0.0 copy-done.3
  2.2 0.0 copy-start
  2.2 1.0 %copy-done = f32[1,4,4,2,16,256]{5,4,3,2,1,0:T(8,128)S(1)} copy-done((f32[1,4,4,2,16,256]{5,4,3,2,1,0:T(8,128)S(1)}, f32[1,4,4,2,16,256]{5,4,3,2,1,0:T(8,128)}, u32[]{:S(2)}) %copy-start) | copy-done | bytes 524312
  3.2 0.0 copy-start.1
  3.2 0.9 %copy-done.1 = f32[1,4,2,16,256]{4,3,2,1,0:T(8,128)S(1)} copy-done((f32[1,4,2,16,256]{4,3,2,1,0:T(8,128)S(1)}, f32[1,4,2,16,256]{4,3,2,1,0:T(8,128)}, u32[]{:S(2)}) %copy-start.1) | copy-done | bytes 131096
  4.1 0.0 copy-start.2
  4.1 0.9 %copy-done.2 = f32[1,4,2,16,256]{4,3,2,1,0:T(8,128)S(1)} copy-done((f32[1,4,2,16,256]{4,3,2,1,0:T(8,128)S(1)}, f32[1,4,2,16,256]{4,3,2,1,0:T(8,128)}, u32[]{:S(2)}) %copy-start.2) | copy-done | bytes 131096
  5.0 44.1 %shard_map.86 = (f32[4,2,16,256]{3,2,1,0:T(8,128)S(1)}, f32[4,8,128]{2,1,0:T(8,128)S(1)}) custom-call(f32[4,2,16,256]{3,2,1,0:T(8,128)S(1)} %bitcast.13, f32[4,2,16,256]{3,2,1,0:T(8,128)S(1)} %bitcast.14, f32[2,16,256]{2,1,0:T(8,128)S(1)} %bitcast.16, f32[4,4,2,16,256]{4,3,2,1,0:T(8,128)S(1)} %bitcast.11, s32[64,4]{1,0:T(8,128)S(1)} %bitcast.12, ...), custom_call_target="tpu_custom_call" | custom-call | flops 8000000 | bytes 1000000 | tf_op jit(solution)/shard_map/pallas_call | solution.py:444
  49.1 0.7 %copy.15 = f32[1,4,2,16,256]{4,3,2,1,0:T(8,128)} copy(f32[1,4,2,16,256]{4,3,2,1,0:T(8,128)S(1)} %bitcast.15) | data formatting | bytes 262144
  49.8 0.6 %copy.16 = f32[1,4,1,8,128]{4,3,2,1,0:T(8,128)} copy(f32[1,4,1,8,128]{4,3,2,1,0:T(8,128)S(1)} %bitcast.17) | data formatting | bytes 32768
Async XLA Ops:
  0.6 0.7 %copy-start.4 = (s32[1,1,32,4]{2,3,1,0:T(4,128)S(1)}, s32[1,1,32,4]{2,3,1,0:T(4,128)}, u32[]{:S(2)}) copy-start(s32[1,1,32,4]{2,3,1,0:T(4,128)} %param.12) | copy-start | bytes 1540
  0.6 0.8 %copy-start.5 = (f32[1,1,32,4]{2,3,1,0:T(4,128)S(1)}, f32[1,1,32,4]{2,3,1,0:T(4,128)}, u32[]{:S(2)}) copy-start(f32[1,1,32,4]{2,3,1,0:T(4,128)} %param.13) | copy-start | bytes 1540
  1.3 0.9 %copy-start.3 = (f32[1,2,16,256]{3,2,1,0:T(8,128)S(1)}, f32[1,2,16,256]{3,2,1,0:T(8,128)}, u32[]{:S(2)}) copy-start(f32[1,2,16,256]{3,2,1,0:T(8,128)} %param.9) | copy-start | bytes 98308
  1.4 0.7 %copy-start.6 = (s32[1,1,64,4]{2,3,1,0:T(4,128)S(1)}, s32[1,1,64,4]{2,3,1,0:T(4,128)}, u32[]{:S(2)}) copy-start(s32[1,1,64,4]{2,3,1,0:T(4,128)} %param.11) | copy-start | bytes 3076
  2.2 1.0 %copy-start = (f32[1,4,4,2,16,256]{5,4,3,2,1,0:T(8,128)S(1)}, f32[1,4,4,2,16,256]{5,4,3,2,1,0:T(8,128)}, u32[]{:S(2)}) copy-start(f32[1,4,4,2,16,256]{5,4,3,2,1,0:T(8,128)} %param.10) | copy-start | bytes 1572868
  3.2 0.9 %copy-start.1 = (f32[1,4,2,16,256]{4,3,2,1,0:T(8,128)S(1)}, f32[1,4,2,16,256]{4,3,2,1,0:T(8,128)}, u32[]{:S(2)}) copy-start(f32[1,4,2,16,256]{4,3,2,1,0:T(8,128)} %param.7) | copy-start | bytes 393220
  4.1 0.9 %copy-start.2 = (f32[1,4,2,16,256]{4,3,2,1,0:T(8,128)S(1)}, f32[1,4,2,16,256]{4,3,2,1,0:T(8,128)}, u32[]{:S(2)}) copy-start(f32[1,4,2,16,256]{4,3,2,1,0:T(8,128)} %param.8) | copy-start | bytes 393220

commit v2 on v1

--- a/solution.py
+++ b/solution.py
@@ -28,7 +28,7 @@
     strips, layers,
     iterate_hbm, forcing_hbm, eta_hbm, inverse_hbm, cells_hbm, slots_hbm, weights_hbm,
     iterate_out, coarse_out,
-    cur, frc, eta, vin, cel, slt, wgt,
+    cur, frc, eta, vin, cel, slt, wgt, takes,
     onehot, pick, pick_edge, weigh, diag, w_phi, w_lat, w_rad, inv_eta, gain, edge_w, edge_ie,
     rim_send, rim_recv, rad_recv, phi_send, phi_recv,
     eta_rad, eta_phi_send, eta_phi, ceta, ceta_rad, cdia, cfaces,
@@ -38,29 +38,36 @@
     patch, lat, rad = lax.axis_index("patch"), lax.axis_index("lat"), lax.axis_index("rad")
     _, _, width, na = frc.shape
     half = na // 2
-    below = (patch, lat, lax.rem(rad + layers - 1, layers))
-    above = (patch, lat, lax.rem(rad + 1, layers))
-    left = (patch, lax.rem(lat + strips - 1, strips), rad)
-    right = (patch, lax.rem(lat + 1, strips), rad)
     has_below, has_above = rad > 0, rad < layers - 1
     has_left, has_right = lat > 0, lat < strips - 1
 
+    def neighbour(has, lat_step, rad_step):
+        return (
+            jnp.where(has, patch, 1 - patch),
+            jnp.where(has, lat + lat_step, lat),
+            jnp.where(has, rad + rad_step, rad),
+        )
+
+    below, above = neighbour(has_below, 0, -1), neighbour(has_above, 0, 1)
+    left, right = neighbour(has_left, -1, 0), neighbour(has_right, 1, 0)
+    at_above, at_right = jnp.where(has_above, 0, 1), jnp.where(has_right, 0, 1)
+    at_below, at_left = jnp.where(has_below, 1, 0), jnp.where(has_left, 1, 0)
+
     def across(offset):
         return (1 - patch, lax.rem(lat + offset + strips, strips), rad)
 
     loads = [
         pltpu.make_async_copy(iterate_hbm, cur.at[0], local_sem.at[0]),
-        pltpu.make_async_copy(cells_hbm, cel.at[pl.ds(0, strips)], local_sem.at[1]),
-        pltpu.make_async_copy(cells_hbm, cel.at[pl.ds(strips, strips)], local_sem.at[2]),
-        pltpu.make_async_copy(eta_hbm, eta, local_sem.at[3]),
-        pltpu.make_async_copy(slots_hbm, slt, local_sem.at[4]),
-        pltpu.make_async_copy(weights_hbm, wgt, local_sem.at[5]),
-        pltpu.make_async_copy(forcing_hbm, frc, local_sem.at[6]),
+        pltpu.make_async_copy(cells_hbm, cel, local_sem.at[1]),
+        pltpu.make_async_copy(eta_hbm, eta, local_sem.at[2]),
+        pltpu.make_async_copy(slots_hbm, slt, local_sem.at[3]),
+        pltpu.make_async_copy(weights_hbm, wgt, local_sem.at[4]),
+        pltpu.make_async_copy(forcing_hbm, frc, local_sem.at[5]),
     ]
     for i in range(4):
         loads.append(
             pltpu.make_async_copy(
-                inverse_hbm.at[i, pl.ds(i, 4 - i)], vin.at[i, pl.ds(i, 4 - i)], local_sem.at[7 + i]
+                inverse_hbm.at[i, pl.ds(i, 4 - i)], vin.at[i, pl.ds(i, 4 - i)], local_sem.at[6 + i]
             )
         )
     for load in loads:
@@ -76,23 +83,34 @@
     for device in (below, above, left, right):
         greet(device)
 
-    def remote(src, dst, sem, device):
+    def remote(src, dst, sem, device, landing=None):
         return pltpu.make_async_remote_copy(
-            src_ref=src, dst_ref=dst, send_sem=send_sem.at[sem], recv_sem=recv_sem.at[sem],
+            src_ref=src, dst_ref=dst, send_sem=send_sem.at[sem],
+            recv_sem=recv_sem.at[sem if landing is None else landing],
             device_id=device, device_id_type=pl.DeviceIdType.MESH,
         )
 
+    def pair(src_up, src_down, dst, sem, up, down, at_up, at_down):
+        return [
+            remote(src_up, dst.at[at_up], sem, up, sem + at_up),
+            remote(src_down, dst.at[at_down], sem + 1, down, sem + at_down),
+        ]
+
+    def rad_pair(src_up, src_down, dst, sem):
+        return pair(src_up, src_down, dst, sem, above, below, at_above, at_below)
+
+    def phi_pair(src, dst, sem):
+        return pair(src.at[0], src.at[1], dst, sem, right, left, at_right, at_left)
+
+    def arrived(dst, sem):
+        for side in range(2):
+            pltpu.make_async_copy(dst.at[side], dst.at[side], recv_sem.at[sem + side]).wait()
+
     def rad_copies(k):
-        return [
-            remote(cur.at[k, :, 1], rad_recv.at[k, 0], RAD + 2 * k, above),
-            remote(cur.at[k, :, 0], rad_recv.at[k, 1], RAD + 2 * k + 1, below),
-        ]
+        return rad_pair(cur.at[k, :, 1], cur.at[k, :, 0], rad_recv.at[k], RAD + 2 * k)
 
     def phi_copies(k):
-        return [
-            remote(phi_send.at[k, 0], phi_recv.at[k, 0], PHI + 2 * k, right),
-            remote(phi_send.at[k, 1], phi_recv.at[k, 1], PHI + 2 * k + 1, left),
-        ]
+        return phi_pair(phi_send.at[k], phi_recv.at[k], PHI + 2 * k)
 
     def rim_start(k):
         for slot in sorted(range(WIN), key=lambda s: -abs(s - WIN // 2 + 1)):
@@ -104,20 +122,12 @@
     def rim_all(k, sem):
         return pltpu.make_async_copy(rim_recv.at[k], rim_recv.at[k], sem.at[RIM + k])
 
-    eta_copies = [
-        remote(eta.at[1], eta_rad.at[0], ETA_RAD, above),
-        remote(eta.at[0], eta_rad.at[1], ETA_RAD + 1, below),
-        remote(ceta, ceta_rad.at[0], COARSE_RAD, above),
-        remote(ceta, ceta_rad.at[1], COARSE_RAD + 1, below),
-        remote(eta_phi_send.at[0], eta_phi.at[0], ETA_PHI, right),
-        remote(eta_phi_send.at[1], eta_phi.at[1], ETA_PHI + 1, left),
-    ]
-    first_copies = [
-        remote(first, first_rad.at[0], FIRST_RAD, above),
-        remote(first, first_rad.at[1], FIRST_RAD + 1, below),
-        remote(first_phi_send.at[0], first_phi.at[0], FIRST_PHI, right),
-        remote(first_phi_send.at[1], first_phi.at[1], FIRST_PHI + 1, left),
-    ]
+    eta_copies = (
+        rad_pair(eta.at[1], eta.at[0], eta_rad, ETA_RAD)
+        + rad_pair(ceta, ceta, ceta_rad, COARSE_RAD)
+        + phi_pair(eta_phi_send, eta_phi, ETA_PHI)
+    )
+    first_copies = phi_pair(first_phi_send, first_phi, FIRST_PHI) + rad_pair(first, first, first_rad, FIRST_RAD)
 
     def iota(shape, dim):
         return lax.broadcasted_iota(jnp.int32, shape, dim)
@@ -158,13 +168,14 @@
     rim_send[...] = jnp.zeros_like(rim_send)
     eta_phi_send[...] = jnp.zeros_like(eta_phi_send)
     loads[1].wait()
-    loads[2].wait()
-    mine = cel[pl.ds(lax.rem(lat + strips - WIN // 2 + 1, strips), WIN), :].astype(F32)
-    lanes = iota((WIN, WIN * CAP), 1)
-    spread = jnp.zeros((WIN, WIN * CAP), F32)
+    cells = cel[...].astype(F32)
+    cells = jnp.concatenate([cells, cells], axis=1)
+    spread = jnp.zeros((CAP, WIN * CAP), F32)
+    begin = lat + strips - WIN // 2 + 1
     for s in range(CAP):
-        spread = jnp.where(lanes // WIN == s, mine[:, s : s + 1], spread)
-    spread = jnp.where(lanes % WIN == iota((WIN, WIN * CAP), 0), spread, 0.0)
+        here = (iota((CAP, WIN * CAP), 1) // WIN == s) & (iota((CAP, WIN * CAP), 0) == s)
+        turn = lax.rem(WIN * s - begin + 4 * strips, 2 * strips)
+        spread = jnp.where(here, pltpu.roll(cells, turn, 1), spread)
     cell = jnp.sum(spread, axis=0, keepdims=True).astype(jnp.int32)
     cell_lat, cell_lon = cell % na, cell // na
     onehot[...] = (iota((na, WIN * CAP), 0) == cell_lat).astype(F32).astype(jnp.bfloat16)
@@ -176,7 +187,7 @@
     put_rim(0, pack(cur[0].reshape(8 * width, na)))
     put_edges(0)
 
-    loads[3].wait()
+    loads[2].wait()
     fold[0:width, :] = exact_dot(eta[0] + eta[1], pairs)
     coarse_eta = 0.125 * fold_rows(width // 2)
     ceta[...] = coarse_eta
@@ -191,17 +202,22 @@
     for copy in rad_copies(0) + phi_copies(0) + eta_copies:
         copy.start()
 
-    for load in loads[4:]:
+    for load in loads[3:]:
         load.wait()
+    takes[...] = jnp.zeros_like(takes)
+    takes[0:4, 0 : 2 * width] = slt[...].astype(F32)
+    takes[4:8, 0 : 2 * width] = wgt[...]
+    columns = takes[...].T[0 : 2 * width]
     lanes = iota((2 * width, WIN * CAP), 1)
-    slot_here = lax.rem(lanes % WIN + lat + strips - WIN // 2, strips) * CAP + lanes // WIN
+    slot_here = (lax.rem(lanes % WIN + lat + strips - WIN // 2, strips) * CAP + lanes // WIN).astype(F32)
     total = jnp.zeros((2 * width, WIN * CAP), F32)
     for s in range(4):
-        total = total + jnp.where(slt[:, s : s + 1] == slot_here, wgt[:, s : s + 1], 0.0)
+        total = total + jnp.where(columns[:, s : s + 1] == slot_here, columns[:, 4 + s : 5 + s], 0.0)
     weigh[...] = total
 
-    for copy in eta_copies:
-        copy.wait_recv()
+    arrived(eta_rad, ETA_RAD)
+    arrived(ceta_rad, COARSE_RAD)
+    arrived(eta_phi, ETA_PHI)
     eta_below = jnp.where(has_below, eta_rad[0], 0.0)
     eta_above = jnp.where(has_above, eta_rad[1], 0.0)
     w_rad[0] = 0.5 * (eta[0] + eta_below)
@@ -277,8 +293,7 @@
             else:
                 result[0][r] = result[0][r] + 0.5 * other[3]
                 flows[r] = flows[r] - other[0]
-        for copy in phi_copies(k):
-            copy.wait_recv()
+        arrived(phi_recv.at[k], PHI + 2 * k)
         for r in range(2):
             lo, hi = [], []
             for c in range(4):
@@ -291,8 +306,7 @@
             result[1][r] = result[1][r] + 0.5 * (lo[3] - hi[3])
             sums[r] = sums[r] + lo[3] + hi[3]
             flows[r] = flows[r] + (hi[1] - lo[1])
-        for copy in rad_copies(k):
-            copy.wait_recv()
+        arrived(rad_recv.at[k], RAD + 2 * k)
         for r in range(2):
             has, sign, w = (has_below, 0.5, w_rad[0]) if r == 0 else (has_above, -0.5, w_rad[2])
             n = [jnp.where(has, rad_recv[k, r, c], 0.0) for c in range(4)]
@@ -388,8 +402,8 @@
     one = [first[c] for c in range(4)]
     lat_lo = [shift(one[c], 1, False, 0.0) for c in range(4)]
     lat_hi = [shift(one[c], 1, True, 0.0) for c in range(4)]
-    for copy in first_copies:
-        copy.wait_recv()
+    arrived(first_phi, FIRST_PHI)
+    arrived(first_rad, FIRST_RAD)
     low, high = [], []
     low.append([jnp.where(has_below, first_rad[0, c], 0.0) for c in range(4)])
     high.append([jnp.where(has_above, first_rad[1, c], 0.0) for c in range(4)])
@@ -427,7 +441,7 @@
 
     scratch = [
         vmem(rounds, *field), vmem(*field), vmem(radial, width, na), vmem(4, *field),
-        vmem(2 * strips, CAP, dtype=jnp.int32), vmem(2 * width, 4, dtype=jnp.int32), vmem(2 * width, 4),
+        vmem(CAP, strips, dtype=jnp.int32), vmem(4, 2 * width, dtype=jnp.int32), vmem(4, 2 * width), vmem(8, 128),
         vmem(na, slots, dtype=jnp.bfloat16), vmem(width, slots), vmem(2, width, slots), vmem(2 * width, slots),
         vmem(radial, width, na), vmem(2, radial, width, na), vmem(2, radial, width, na), vmem(3, width, na),
         vmem(radial, width, na), vmem(2, 4, 4, radial, width, half), vmem(2, radial, width, half),
@@ -441,21 +455,23 @@
         pltpu.SemaphoreType.DMA((11,)), pltpu.SemaphoreType.DMA((30,)), pltpu.SemaphoreType.DMA((30,)),
     ]
     anywhere = pl.BlockSpec(memory_space=pl.ANY)
+    whole = pl.BlockSpec(memory_space=pltpu.HBM)
     iterate, coarse = pl.pallas_call(
         functools.partial(kernel, strips, layers),
         out_shape=(
             jax.ShapeDtypeStruct(field, F32),
             jax.ShapeDtypeStruct((comps, width // 2, half), F32),
         ),
-        in_specs=[anywhere] * 7,
+        in_specs=[whole] * 7,
         out_specs=(anywhere, pl.BlockSpec(memory_space=pltpu.VMEM)),
         scratch_shapes=scratch,
         compiler_params=pltpu.CompilerParams(
-            collective_id=0, has_side_effects=True, vmem_limit_bytes=32 * 1024 * 1024
+            collective_id=0, has_side_effects=True, vmem_limit_bytes=60 * 1024 * 1024
         ),
         cost_estimate=pl.CostEstimate(flops=8_000_000, bytes_accessed=1_000_000, transcendentals=0),
     )(
-        iterate_in[0], forcing[0], viscosity[0], vanka_inverse[0], pack_cells[0, 0], take_slot[0, 0], take_weight[0, 0],
+        iterate_in[0], forcing[0], viscosity[0], vanka_inverse[0],
+        pack_cells[0, 0].T, take_slot[0, 0].T, take_weight[0, 0].T,
     )
     return iterate[None], coarse[None, :, None]
 

time: 50.7 us -> 44.6 us (0.88)
  local copies, waits for them, and re-layouts: 5.64 us -> 2.18 us
  Pallas kernels: 44.1 us -> 41.6 us
    unnamed x17 -> x4, local copies, waits for them, and re-layouts: 5.47 us -> 2.18 us
    pallas_call x1, Pallas kernels: 44.1 us -> 41.6 us  [shards(): pl.pallas_call(functools.partial(kernel, strips, layers), out_shape=(jax....]
where the time goes in v2:
time: 44.6 us; the launch traced here: 44.4 us
  Pallas kernels  41.6 us (93%)
  local copies, waits for them, and re-layouts  2.18 us (5%)
  between operations  0.65 us (1%)
    pallas_call x1, Pallas kernels, shards(): pl.pallas_call(functools.partial(kernel, strips, layers), out_shape=(jax....  41.6 us
    unnamed x4, local copies, waits for them, and re-layouts  2.18 us

profile of v2, /device:TPU:1, one launch (start us, length us, event | category | flops | bytes accessed | tf_op | source)
XLA Modules:
  0.0 44.4 jit_solution(17316883477535897672)
XLA Ops:
  0.6 41.6 %shard_map.86 = (f32[4,2,16,256]{3,2,1,0:T(8,128)}, f32[4,8,128]{2,1,0:T(8,128)}) custom-call(f32[4,2,16,256]{3,2,1,0:T(8,128)} %bitcast.18, f32[4,2,16,256]{3,2,1,0:T(8,128)} %bitcast.19, f32[2,16,256]{2,1,0:T(8,128)} %bitcast.21, f32[4,4,2,16,256]{4,3,2,1,0:T(8,128)} %bitcast.17, s32[4,64]{1,0:T(4,128)} %bitcast.23, s32[4,32]{1,0:T(4,128)} %bitcast.24, ...), custom_call_target="tpu_custom_call" | custom-call | flops 8000000 | bytes 1000000 | tf_op jit(solution)/shard_map/pallas_call | solution.py:459
  42.2 0.0 copy-start
  42.2 1.6 %copy.12 = f32[1,4,2,16,256]{4,3,2,1,0:T(8,128)} copy(f32[1,4,2,16,256]{4,3,2,1,0:T(8,128)} %bitcast.20) | data formatting | bytes 262144
  43.8 0.0 copy-done
  43.8 0.6 %copy.13 = f32[1,4,1,8,128]{4,3,2,1,0:T(8,128)} copy(f32[1,4,1,8,128]{4,3,2,1,0:T(8,128)S(1)} %bitcast.22) | data formatting | bytes 32768
Async XLA Ops:
  42.2 1.6 %copy-start = (f32[4,8,128]{2,1,0:T(8,128)S(1)}, f32[4,8,128]{2,1,0:T(8,128)}, u32[]{:S(2)}) copy-start(f32[4,8,128]{2,1,0:T(8,128)} %get-tuple-element.5) | copy-start | bytes 49156

commit v3 on v2

--- a/solution.py
+++ b/solution.py
@@ -429,6 +429,17 @@
     store.wait()
 
 
+def write_out(iterate, coarse, iterate_out, coarse_out, sem):
+    copies = [
+        pltpu.make_async_copy(iterate, iterate_out, sem.at[0]),
+        pltpu.make_async_copy(coarse, coarse_out, sem.at[1]),
+    ]
+    for copy in copies:
+        copy.start()
+    for copy in copies:
+        copy.wait()
+
+
 def shards(strips, layers, iterate_in, forcing, viscosity, vanka_inverse, pack_cells, take_slot, take_weight):
     _, comps, radial, width, na = iterate_in.shape
     half = na // 2
@@ -459,11 +470,11 @@
     iterate, coarse = pl.pallas_call(
         functools.partial(kernel, strips, layers),
         out_shape=(
-            jax.ShapeDtypeStruct(field, F32),
-            jax.ShapeDtypeStruct((comps, width // 2, half), F32),
+            pltpu.VMEM(field, F32),
+            pltpu.VMEM((comps, width // 2, half), F32),
         ),
         in_specs=[whole] * 7,
-        out_specs=(anywhere, pl.BlockSpec(memory_space=pltpu.VMEM)),
+        out_specs=(pl.BlockSpec(memory_space=pltpu.VMEM),) * 2,
         scratch_shapes=scratch,
         compiler_params=pltpu.CompilerParams(
             collective_id=0, has_side_effects=True, vmem_limit_bytes=60 * 1024 * 1024
@@ -473,6 +484,16 @@
         iterate_in[0], forcing[0], viscosity[0], vanka_inverse[0],
         pack_cells[0, 0].T, take_slot[0, 0].T, take_weight[0, 0].T,
     )
+    iterate, coarse = pl.pallas_call(
+        write_out,
+        out_shape=(
+            jax.ShapeDtypeStruct(field, F32),
+            jax.ShapeDtypeStruct((comps, width // 2, half), F32),
+        ),
+        in_specs=[pl.BlockSpec(memory_space=pltpu.VMEM)] * 2,
+        out_specs=(whole, whole),
+        scratch_shapes=[pltpu.SemaphoreType.DMA((2,))],
+    )(*(pltpu.with_memory_space_constraint(x, pltpu.VMEM) for x in (iterate, coarse)))
     return iterate[None], coarse[None, :, None]
 
 

time: 44.6 us -> 42.5 us (0.953)
  local copies, waits for them, and re-layouts: 2.18 us -> 0 us
    unnamed x4 -> x0, local copies, waits for them, and re-layouts: 2.18 us -> none
    pallas_call x1 -> x2, Pallas kernels: 41.6 us -> 41.7 us  [the longest x1 41 us: shards(): pl.pallas_call(functools.partial(kernel, strips, layers), out_shape=(pltp...]
where the time goes in v3:
time: 42.5 us; the launch traced here: 42.3 us
  Pallas kernels  41.7 us (98%)
  between operations  0.64 us (2%)
    pallas_call x1, Pallas kernels, shards(): pl.pallas_call(functools.partial(kernel, strips, layers), out_shape=(pltp...  41 us

profile of v3, /device:TPU:1, one launch (start us, length us, event | category | flops | bytes accessed | tf_op | source)
XLA Modules:
  0.0 42.3 jit_solution(986450887341949139)
XLA Ops:
  0.6 41.0 %shard_map.86 = (f32[4,2,16,256]{3,2,1,0:T(8,128)S(1)}, f32[4,8,128]{2,1,0:T(8,128)S(1)}) custom-call(f32[4,2,16,256]{3,2,1,0:T(8,128)} %bitcast.18, f32[4,2,16,256]{3,2,1,0:T(8,128)} %bitcast.19, f32[2,16,256]{2,1,0:T(8,128)} %bitcast.20, f32[4,4,2,16,256]{4,3,2,1,0:T(8,128)} %bitcast.17, s32[4,64]{1,0:T(4,128)} %bitcast.21, s32[4,32]{1,0:T(4,128)} %bitcast.22, ...), custom_call_target="tpu_custom_call" | custom-call | flops 8000000 | bytes 1000000 | tf_op jit(solution)/shard_map/pallas_call | solution.py:470
  41.6 0.7 %shard_map.87 = (f32[4,2,16,256]{3,2,1,0:T(8,128)}, f32[4,8,128]{2,1,0:T(8,128)}) custom-call(f32[4,2,16,256]{3,2,1,0:T(8,128)S(1)} %get-tuple-element.6.iterate, f32[4,8,128]{2,1,0:T(8,128)S(1)} %get-tuple-element.7.coarse), custom_call_target="tpu_custom_call" | custom-call | tf_op jit(solution)/shard_map/pallas_call | solution.py:487

commit v4 on v3

--- a/solution.py
+++ b/solution.py
@@ -28,8 +28,8 @@
     strips, layers,
     iterate_hbm, forcing_hbm, eta_hbm, inverse_hbm, cells_hbm, slots_hbm, weights_hbm,
     iterate_out, coarse_out,
-    cur, frc, eta, vin, cel, slt, wgt, takes,
-    onehot, pick, pick_edge, weigh, diag, w_phi, w_lat, w_rad, inv_eta, gain, edge_w, edge_ie,
+    cur, frc, eta, vin, cel, slt, wgt,
+    onehot, pick, pick_edge, take_at, take_by, slot_gain, diag, w_phi, w_lat, w_rad, inv_eta, gain, edge_w, edge_ie,
     rim_send, rim_recv, rad_recv, phi_send, phi_recv,
     eta_rad, eta_phi_send, eta_phi, ceta, ceta_rad, cdia, cfaces,
     first, first_rad, first_phi_send, first_phi, fold,
@@ -160,10 +160,13 @@
                 phi_send[k, 0, 2 * c + r, :] = cur[k, c, r, width - 1, :]
                 phi_send[k, 1, 2 * c + r, :] = cur[k, c, r, 0, :]
 
+    def take(x, index):
+        return jnp.take_along_axis(x, index, axis=1, mode="promise_in_bounds")
+
     pairs = (iota((na, half), 0) // 2 == iota((na, half), 1)).astype(F32).astype(jnp.bfloat16)
 
-    def fold_rows(count):
-        return fold[pl.ds(0, count, stride=2), :] + fold[pl.ds(1, count, stride=2), :]
+    def fold_rows(n, count):
+        return fold[n, pl.ds(0, count, stride=2), :] + fold[n, pl.ds(1, count, stride=2), :]
 
     rim_send[...] = jnp.zeros_like(rim_send)
     eta_phi_send[...] = jnp.zeros_like(eta_phi_send)
@@ -188,8 +191,8 @@
     put_edges(0)
 
     loads[2].wait()
-    fold[0:width, :] = exact_dot(eta[0] + eta[1], pairs)
-    coarse_eta = 0.125 * fold_rows(width // 2)
+    fold[0, 0:width, :] = exact_dot(eta[0] + eta[1], pairs)
+    coarse_eta = 0.125 * fold_rows(0, width // 2)
     ceta[...] = coarse_eta
     for r in range(2):
         eta_phi_send[0, r, :] = eta[r, width - 1, :]
@@ -197,45 +200,32 @@
     eta_phi_send[0, 2, 0:half] = ceta[width // 2 - 1, :]
     eta_phi_send[1, 2, 0:half] = ceta[0, :]
 
-    pl.semaphore_wait(barrier, WIN + 4)
-    rim_start(0)
-    for copy in rad_copies(0) + phi_copies(0) + eta_copies:
-        copy.start()
-
     for load in loads[3:]:
         load.wait()
-    takes[...] = jnp.zeros_like(takes)
-    takes[0:4, 0 : 2 * width] = slt[...].astype(F32)
-    takes[4:8, 0 : 2 * width] = wgt[...]
-    columns = takes[...].T[0 : 2 * width]
-    lanes = iota((2 * width, WIN * CAP), 1)
-    slot_here = (lax.rem(lanes % WIN + lat + strips - WIN // 2, strips) * CAP + lanes // WIN).astype(F32)
-    total = jnp.zeros((2 * width, WIN * CAP), F32)
-    for s in range(4):
-        total = total + jnp.where(columns[:, s : s + 1] == slot_here, columns[:, 4 + s : 5 + s], 0.0)
-    weigh[...] = total
-
-    arrived(eta_rad, ETA_RAD)
-    arrived(ceta_rad, COARSE_RAD)
-    arrived(eta_phi, ETA_PHI)
-    eta_below = jnp.where(has_below, eta_rad[0], 0.0)
-    eta_above = jnp.where(has_above, eta_rad[1], 0.0)
-    w_rad[0] = 0.5 * (eta[0] + eta_below)
-    w_rad[1] = 0.5 * (eta[0] + eta[1])
-    w_rad[2] = 0.5 * (eta[1] + eta_above)
+    slot = slt[...]
+    strip = lax.rem(slot // CAP - lat + WIN // 2 + 2 * strips, strips)
+    at = ((slot % CAP) * WIN + strip).astype(F32)
+    idle = jnp.zeros((4, WIN * CAP - 2 * width), F32)
+    at, by = jnp.concatenate([at, idle], axis=1), jnp.concatenate([wgt[...], idle], axis=1)
+    table = jnp.concatenate([at, by], axis=0)
+    beside_low, beside_high = cell_lat == 0, cell_lat == na - 1
+    beside_at = jnp.where(beside_low, cell_lon, jnp.where(beside_high, cell_lon + width, 0))
+    moved = take(table, jnp.broadcast_to(beside_at, (8, WIN * CAP)))
+    for which, rows in ((0, table), (1, moved)):
+        for n in range(4):
+            take_at[which, n] = jnp.broadcast_to(rows[n : n + 1], (8, WIN * CAP)).astype(jnp.int32)
+            weight = rows[4 + n : 5 + n]
+            if which == 1:
+                weight = jnp.where(beside_low | beside_high, weight, 0.0)
+            take_by[which, n] = jnp.broadcast_to(weight, (8, WIN * CAP))
+
     for r in range(2):
         own = eta[r]
-        low_row = jnp.where(has_left, eta_phi[0, r : r + 1, :], 0.0)
-        high_row = jnp.where(has_right, eta_phi[1, r : r + 1, :], 0.0)
-        phi_low = 0.5 * (own + shift(own, 0, False, low_row))
-        phi_high = 0.5 * (own + shift(own, 0, True, high_row))
         lat_low = 0.5 * (own + shift(own, 1, False, own))
         lat_high = 0.5 * (own + shift(own, 1, True, own))
         inverse_eta = 1.0 / own
-        w_phi[0, r], w_phi[1, r] = phi_low, phi_high
         w_lat[0, r], w_lat[1, r] = lat_low, lat_high
         inv_eta[r] = inverse_eta
-        diag[r] = w_rad[r] + w_rad[r + 1] + (phi_low + phi_high) + (lat_low + lat_high)
         for e in range(2):
             at = 0 if e == 0 else na - 1
 
@@ -252,24 +242,35 @@
                 gain[e, i, 1, r] = v[1] * w
                 gain[e, i, 2, r] = v[2] * w - sign * v[3]
                 gain[e, i, 3, r] = v[3] * ie + sign * v[2]
-
-    own = ceta[...]
-    c_below = jnp.where(has_below, ceta_rad[0], 0.0)
-    c_above = jnp.where(has_above, ceta_rad[1], 0.0)
-    c_left = jnp.where(has_left, eta_phi[0, 2:3, 0:half], 0.0)
-    c_right = jnp.where(has_right, eta_phi[1, 2:3, 0:half], 0.0)
-    faces = [
-        0.5 * (own + c_below), 0.5 * (own + c_above),
-        0.5 * (own + shift(own, 0, False, c_left)), 0.5 * (own + shift(own, 0, True, c_right)),
-        0.5 * (own + shift(own, 1, False, own)), 0.5 * (own + shift(own, 1, True, own)),
-    ]
-    for n, face in enumerate(faces):
-        cfaces[n] = face
-    faces_sum = (faces[0] + faces[1]) + (faces[2] + faces[3]) + (faces[4] + faces[5])
-    cdia[0] = faces_sum
-    cdia[1] = OMEGA / (0.25 * faces_sum)
-    cdia[2] = OMEGA / (0.25 * (6.0 / own))
-    cdia[3] = 1.0 / own
+    w_rad[1] = 0.5 * (eta[0] + eta[1])
+    for d in range(4):
+        rows = []
+        for i in range(4):
+            for r in range(2):
+                j = (i + d) % 4
+                rows.append(gain[0, i, j, r] * pick_edge[0] + gain[1, i, j, r] * pick_edge[1])
+        slot_gain[d] = jnp.sum(jnp.stack(rows, axis=0), axis=1)
+
+    pl.semaphore_wait(barrier, WIN + 4)
+    rim_start(0)
+    for copy in eta_copies + phi_copies(0) + rad_copies(0):
+        copy.start()
+
+    arrived(eta_rad, ETA_RAD)
+    arrived(ceta_rad, COARSE_RAD)
+    arrived(eta_phi, ETA_PHI)
+    eta_below = jnp.where(has_below, eta_rad[0], 0.0)
+    eta_above = jnp.where(has_above, eta_rad[1], 0.0)
+    w_rad[0] = 0.5 * (eta[0] + eta_below)
+    w_rad[2] = 0.5 * (eta[1] + eta_above)
+    for r in range(2):
+        own = eta[r]
+        low_row = jnp.where(has_left, eta_phi[0, r : r + 1, :], 0.0)
+        high_row = jnp.where(has_right, eta_phi[1, r : r + 1, :], 0.0)
+        phi_low = 0.5 * (own + shift(own, 0, False, low_row))
+        phi_high = 0.5 * (own + shift(own, 0, True, high_row))
+        w_phi[0, r], w_phi[1, r] = phi_low, phi_high
+        diag[r] = w_rad[r] + w_rad[r + 1] + (phi_low + phi_high) + (w_lat[0, r] + w_lat[1, r])
 
     def residual(k):
         result = [[None, None] for _ in range(4)]
@@ -317,11 +318,26 @@
             result[3][r] = frc[3, r] + inv_eta[r] * (sums[r] + n[3]) + 0.5 * flow
         return result
 
-    def ghosts(k):
+    def received(k):
         rim_all(k, recv_sem).wait()
-        turned = rim_recv[k].T
-        by_slot = jnp.concatenate([turned[8 * s : 8 * s + 8] for s in range(CAP)], axis=1)
-        return jnp.sum(by_slot[:, None, :] * weigh[...][None], axis=-1, keepdims=True)
+        turned = jnp.concatenate([rim_recv[k]] * CAP, axis=0).T
+        by_slot = turned[0:8]
+        for s in range(1, CAP):
+            by_slot = jnp.where(slot_lane // WIN == s, turned[8 * s : 8 * s + 8], by_slot)
+        return by_slot
+
+    def interpolate(by_slot, which):
+        terms = [take_by[which, n] * take(by_slot, take_at[which, n]) for n in range(4)]
+        return (terms[0] + terms[1]) + (terms[2] + terms[3])
+
+    def columns_of(ghost):
+        down = iota((8, WIN * CAP), 0)
+        result = []
+        for n in range(8):
+            line = jnp.broadcast_to(ghost[n : n + 1], (8, WIN * CAP))
+            parts = [take(line, down + 8 * m) for m in range(2 * width // 8)]
+            result.append([jnp.concatenate(parts[:2], axis=0), jnp.concatenate(parts[2:], axis=0)])
+        return result
 
     def sent(k):
         for copy in rad_copies(k) + phi_copies(k):
@@ -339,29 +355,31 @@
                 cur[k + 1, i, r] = gained
         packed = pack(cur[k + 1].reshape(8 * width, na))
         sent(k)
-        ghost = ghosts(k)
+        by_slot = received(k)
+        beside = interpolate(by_slot, 1)
+        for d in range(4):
+            turned = beside if d == 0 else pltpu.roll(beside, 8 - 2 * d, 0)
+            packed = packed + slot_gain[d] * turned
+        put_rim(k + 1, packed)
+        rim_start(k + 1)
+        ghost = columns_of(interpolate(by_slot, 0))
         deltas = []
         for e in range(2):
             delta = []
             for i in range(4):
                 for r in range(2):
-                    value = jnp.zeros((width, half), F32)
-                    for j in range(4):
-                        value = value + gain[e, i, j, r] * ghost[2 * j + r, e * width : (e + 1) * width, :]
+                    value = gain[e, i, 0, r] * ghost[r][e]
+                    for j in range(1, 4):
+                        value = value + gain[e, i, j, r] * ghost[2 * j + r][e]
                     delta.append(value)
             deltas.append(delta)
-        at_edge = jnp.stack(
-            [deltas[0][n] * pick_edge[0] + deltas[1][n] * pick_edge[1] for n in range(8)], axis=0
-        )
-        put_rim(k + 1, packed + jnp.sum(at_edge, axis=1))
-        rim_start(k + 1)
         for i in range(4):
             for r in range(2):
                 n = 2 * i + r
                 cur[k + 1, i, r, :, 0:half] += jnp.where(tile_lane == 0, deltas[0][n], 0.0)
                 cur[k + 1, i, r, :, half:na] += jnp.where(tile_lane == half - 1, deltas[1][n], 0.0)
         put_edges(k + 1)
-        for copy in rad_copies(k + 1) + phi_copies(k + 1):
+        for copy in phi_copies(k + 1) + rad_copies(k + 1):
             copy.start()
         return carry
 
@@ -371,24 +389,42 @@
     for copy in eta_copies:
         copy.wait_send()
 
+    own = ceta[...]
+    c_below = jnp.where(has_below, ceta_rad[0], 0.0)
+    c_above = jnp.where(has_above, ceta_rad[1], 0.0)
+    c_left = jnp.where(has_left, eta_phi[0, 2:3, 0:half], 0.0)
+    c_right = jnp.where(has_right, eta_phi[1, 2:3, 0:half], 0.0)
+    faces = [
+        0.5 * (own + c_below), 0.5 * (own + c_above),
+        0.5 * (own + shift(own, 0, False, c_left)), 0.5 * (own + shift(own, 0, True, c_right)),
+        0.5 * (own + shift(own, 1, False, own)), 0.5 * (own + shift(own, 1, True, own)),
+    ]
+    for n, face in enumerate(faces):
+        cfaces[n] = face
+    faces_sum = (faces[0] + faces[1]) + (faces[2] + faces[3]) + (faces[4] + faces[5])
+    cdia[0] = faces_sum
+    cdia[1] = OMEGA / (0.25 * faces_sum)
+    cdia[2] = OMEGA / (0.25 * (6.0 / own))
+    cdia[3] = 1.0 / own
+
     res = residual(SWEEPS)
     summed = jnp.concatenate([res[c][0] + res[c][1] for c in range(4)], axis=0)
-    fold[...] = exact_dot(summed, pairs)
-    base = fold_rows(4 * (width // 2))
+    fold[0] = exact_dot(summed, pairs)
+    base = fold_rows(0, 4 * (width // 2))
     sent(SWEEPS)
-    ghost = ghosts(SWEEPS)
+    ghost = columns_of(interpolate(received(SWEEPS), 0))
     tops = []
     for e in range(2):
         sign = 0.5 if e == 0 else -0.5
         terms = [jnp.zeros((width, half), F32) for _ in range(4)]
         for r in range(2):
-            g = [ghost[2 * j + r, e * width : (e + 1) * width, :] for j in range(4)]
+            g = [ghost[2 * j + r][e] for j in range(4)]
             for c in range(3):
                 terms[c] = terms[c] + edge_w[e, r] * g[c]
             terms[2] = terms[2] + sign * g[3]
             terms[3] = terms[3] + (edge_ie[e, r] * g[3] - sign * g[2])
-        fold[...] = jnp.concatenate(terms, axis=0)
-        tops.append(fold_rows(4 * (width // 2)))
+        fold[1 + e] = jnp.concatenate(terms, axis=0)
+        tops.append(fold_rows(1 + e, 4 * (width // 2)))
     lanes = iota(base.shape, 1)
     coarse = base + jnp.where(lanes == 0, tops[0], 0.0) + jnp.where(lanes == half - 1, tops[1], 0.0)
     coarse = (0.125 * coarse).reshape(4, width // 2, half)
@@ -452,8 +488,9 @@
 
     scratch = [
         vmem(rounds, *field), vmem(*field), vmem(radial, width, na), vmem(4, *field),
-        vmem(CAP, strips, dtype=jnp.int32), vmem(4, 2 * width, dtype=jnp.int32), vmem(4, 2 * width), vmem(8, 128),
-        vmem(na, slots, dtype=jnp.bfloat16), vmem(width, slots), vmem(2, width, slots), vmem(2 * width, slots),
+        vmem(CAP, strips, dtype=jnp.int32), vmem(4, 2 * width, dtype=jnp.int32), vmem(4, 2 * width),
+        vmem(na, slots, dtype=jnp.bfloat16), vmem(width, slots), vmem(2, width, slots),
+        vmem(2, 4, 8, slots, dtype=jnp.int32), vmem(2, 4, 8, slots), vmem(4, 8, slots),
         vmem(radial, width, na), vmem(2, radial, width, na), vmem(2, radial, width, na), vmem(3, width, na),
         vmem(radial, width, na), vmem(2, 4, 4, radial, width, half), vmem(2, radial, width, half),
         vmem(2, radial, width, half),
@@ -462,7 +499,7 @@
         vmem(2, width, na), vmem(2, 8, na), vmem(2, 8, na), vmem(width // 2, half), vmem(2, width // 2, half),
         vmem(4, width // 2, half), vmem(6, width // 2, half),
         vmem(comps, width // 2, half), vmem(2, comps, width // 2, half), vmem(2, comps, half), vmem(2, comps, half),
-        vmem(comps * width, half),
+        vmem(3, comps * width, half),
         pltpu.SemaphoreType.DMA((11,)), pltpu.SemaphoreType.DMA((30,)), pltpu.SemaphoreType.DMA((30,)),
     ]
     anywhere = pl.BlockSpec(memory_space=pl.ANY)

time: 42.5 us -> 42 us (0.988)
  Pallas kernels: 41.7 us -> 41.2 us
    pallas_call x1, Pallas kernels: 41 us -> 40.5 us  [shards(): pl.pallas_call(functools.partial(kernel, strips, layers), out_shape=(pltp...]
where the time goes in v4:
time: 42 us; the launch traced here: 41.8 us
  Pallas kernels  41.2 us (98%)
  between operations  0.64 us (2%)
    pallas_call x1, Pallas kernels, shards(): pl.pallas_call(functools.partial(kernel, strips, layers), out_shape=(pltp...  40.5 us

profile of v4, /device:TPU:1, one launch (start us, length us, event | category | flops | bytes accessed | tf_op | source)
XLA Modules:
  0.0 41.8 jit_solution(13729108814200998243)
XLA Ops:
  0.6 40.5 %shard_map.86 = (f32[4,2,16,256]{3,2,1,0:T(8,128)S(1)}, f32[4,8,128]{2,1,0:T(8,128)S(1)}) custom-call(f32[4,2,16,256]{3,2,1,0:T(8,128)} %bitcast.18, f32[4,2,16,256]{3,2,1,0:T(8,128)} %bitcast.19, f32[2,16,256]{2,1,0:T(8,128)} %bitcast.20, f32[4,4,2,16,256]{4,3,2,1,0:T(8,128)} %bitcast.17, s32[4,64]{1,0:T(4,128)} %bitcast.21, s32[4,32]{1,0:T(4,128)} %bitcast.22, ...), custom_call_target="tpu_custom_call" | custom-call | flops 8000000 | bytes 1000000 | tf_op jit(solution)/shard_map/pallas_call | solution.py:507
  41.2 0.7 %shard_map.87 = (f32[4,2,16,256]{3,2,1,0:T(8,128)}, f32[4,8,128]{2,1,0:T(8,128)}) custom-call(f32[4,2,16,256]{3,2,1,0:T(8,128)S(1)} %get-tuple-element.6.iterate, f32[4,8,128]{2,1,0:T(8,128)S(1)} %get-tuple-element.7.coarse), custom_call_target="tpu_custom_call" | custom-call | tf_op jit(solution)/shard_map/pallas_call | solution.py:524

commit v5 on v4

--- a/solution.py
+++ b/solution.py
@@ -29,7 +29,7 @@
     iterate_hbm, forcing_hbm, eta_hbm, inverse_hbm, cells_hbm, slots_hbm, weights_hbm,
     iterate_out, coarse_out,
     cur, frc, eta, vin, cel, slt, wgt,
-    onehot, pick, pick_edge, take_at, take_by, slot_gain, diag, w_phi, w_lat, w_rad, inv_eta, gain, edge_w, edge_ie,
+    onehot, pick, pick_edge, take_at, take_by, slot_gain, diag, w_phi, w_lat, w_rad, inv_eta, gain, edge_w, edge_ie, edge_gain,
     rim_send, rim_recv, rad_recv, phi_send, phi_recv,
     eta_rad, eta_phi_send, eta_phi, ceta, ceta_rad, cdia, cfaces,
     first, first_rad, first_phi_send, first_phi, fold,
@@ -165,8 +165,8 @@
 
     pairs = (iota((na, half), 0) // 2 == iota((na, half), 1)).astype(F32).astype(jnp.bfloat16)
 
-    def fold_rows(n, count):
-        return fold[n, pl.ds(0, count, stride=2), :] + fold[n, pl.ds(1, count, stride=2), :]
+    def fold_rows(count):
+        return fold[pl.ds(0, count, stride=2), :] + fold[pl.ds(1, count, stride=2), :]
 
     rim_send[...] = jnp.zeros_like(rim_send)
     eta_phi_send[...] = jnp.zeros_like(eta_phi_send)
@@ -191,8 +191,8 @@
     put_edges(0)
 
     loads[2].wait()
-    fold[0, 0:width, :] = exact_dot(eta[0] + eta[1], pairs)
-    coarse_eta = 0.125 * fold_rows(0, width // 2)
+    fold[0:width, :] = exact_dot(eta[0] + eta[1], pairs)
+    coarse_eta = 0.125 * fold_rows(width // 2)
     ceta[...] = coarse_eta
     for r in range(2):
         eta_phi_send[0, r, :] = eta[r, width - 1, :]
@@ -243,6 +243,13 @@
                 gain[e, i, 2, r] = v[2] * w - sign * v[3]
                 gain[e, i, 3, r] = v[3] * ie + sign * v[2]
     w_rad[1] = 0.5 * (eta[0] + eta[1])
+    rows = []
+    for c in range(4):
+        for r in range(2):
+            factors = edge_w if c < 3 else edge_ie
+            low = jnp.where(tile_lane == iota((width, half), 0), factors[0, r], 0.0)
+            rows.append(low + jnp.where(tile_lane == iota((width, half), 0) + width, factors[1, r], 0.0))
+    edge_gain[...] = jnp.sum(jnp.stack(rows, axis=0), axis=1)
     for d in range(4):
         rows = []
         for i in range(4):
@@ -409,25 +416,25 @@
 
     res = residual(SWEEPS)
     summed = jnp.concatenate([res[c][0] + res[c][1] for c in range(4)], axis=0)
-    fold[0] = exact_dot(summed, pairs)
-    base = fold_rows(0, 4 * (width // 2))
+    fold[0 : 4 * width, :] = exact_dot(summed, pairs)
+    base = fold_rows(4 * (width // 2))
     sent(SWEEPS)
-    ghost = columns_of(interpolate(received(SWEEPS), 0))
-    tops = []
-    for e in range(2):
-        sign = 0.5 if e == 0 else -0.5
-        terms = [jnp.zeros((width, half), F32) for _ in range(4)]
-        for r in range(2):
-            g = [ghost[2 * j + r][e] for j in range(4)]
-            for c in range(3):
-                terms[c] = terms[c] + edge_w[e, r] * g[c]
-            terms[2] = terms[2] + sign * g[3]
-            terms[3] = terms[3] + (edge_ie[e, r] * g[3] - sign * g[2])
-        fold[1 + e] = jnp.concatenate(terms, axis=0)
-        tops.append(fold_rows(1 + e, 4 * (width // 2)))
-    lanes = iota(base.shape, 1)
-    coarse = base + jnp.where(lanes == 0, tops[0], 0.0) + jnp.where(lanes == half - 1, tops[1], 0.0)
-    coarse = (0.125 * coarse).reshape(4, width // 2, half)
+    ghost = interpolate(received(SWEEPS), 0)
+    sign = jnp.where(slot_lane < width, 0.5, -0.5)
+    component = iota(ghost.shape, 0) // 2
+    added = edge_gain[...] * ghost
+    added = added + jnp.where(component == 2, sign * pltpu.roll(ghost, 6, 0), 0.0)
+    added = added - jnp.where(component == 3, sign * pltpu.roll(ghost, 2, 0), 0.0)
+    added = added + pltpu.roll(added, 7, 0)
+    down = 2 * iota((width // 2, half), 0)
+    lanes = iota((width // 2, half), 1)
+    coarse = []
+    for c in range(4):
+        line = jnp.broadcast_to(added[2 * c : 2 * c + 1], (width // 2, half))
+        low, high = (take(line, down + e * width) + take(line, down + (e * width + 1)) for e in range(2))
+        total = base[c * (width // 2) : (c + 1) * (width // 2)]
+        total = total + jnp.where(lanes == 0, low, 0.0) + jnp.where(lanes == half - 1, high, 0.0)
+        coarse.append(0.125 * total)
     for c in range(4):
         first[c] = coarse[c] * cdia[1 if c < 3 else 2]
     for c in range(4):
@@ -493,13 +500,13 @@
         vmem(2, 4, 8, slots, dtype=jnp.int32), vmem(2, 4, 8, slots), vmem(4, 8, slots),
         vmem(radial, width, na), vmem(2, radial, width, na), vmem(2, radial, width, na), vmem(3, width, na),
         vmem(radial, width, na), vmem(2, 4, 4, radial, width, half), vmem(2, radial, width, half),
-        vmem(2, radial, width, half),
+        vmem(2, radial, width, half), vmem(8, slots),
         vmem(rounds, WIN, 128), vmem(rounds, WIN, 128), vmem(rounds, 2, comps, width, na),
         vmem(rounds, 2, 2 * comps, na), vmem(rounds, 2, 2 * comps, na),
         vmem(2, width, na), vmem(2, 8, na), vmem(2, 8, na), vmem(width // 2, half), vmem(2, width // 2, half),
         vmem(4, width // 2, half), vmem(6, width // 2, half),
         vmem(comps, width // 2, half), vmem(2, comps, width // 2, half), vmem(2, comps, half), vmem(2, comps, half),
-        vmem(3, comps * width, half),
+        vmem(comps * width + 8, half),
         pltpu.SemaphoreType.DMA((11,)), pltpu.SemaphoreType.DMA((30,)), pltpu.SemaphoreType.DMA((30,)),
     ]
     anywhere = pl.BlockSpec(memory_space=pl.ANY)

time: 42 us -> 41.9 us (level)
  no operation moved by 1% of the time
where the time goes in v5:
time: 41.9 us; the launch traced here: 41.8 us
  Pallas kernels  41.2 us (98%)
  between operations  0.64 us (2%)
    pallas_call x1, Pallas kernels, shards(): pl.pallas_call(functools.partial(kernel, strips, layers), out_shape=(pltp...  40.5 us

profile of v5, /device:TPU:1, one launch (start us, length us, event | category | flops | bytes accessed | tf_op | source)
XLA Modules:
  0.0 41.8 jit_solution(1676672771711263816)
XLA Ops:
  0.6 40.5 %shard_map.86 = (f32[4,2,16,256]{3,2,1,0:T(8,128)S(1)}, f32[4,8,128]{2,1,0:T(8,128)S(1)}) custom-call(f32[4,2,16,256]{3,2,1,0:T(8,128)} %bitcast.18, f32[4,2,16,256]{3,2,1,0:T(8,128)} %bitcast.19, f32[2,16,256]{2,1,0:T(8,128)} %bitcast.20, f32[4,4,2,16,256]{4,3,2,1,0:T(8,128)} %bitcast.17, s32[4,64]{1,0:T(4,128)} %bitcast.21, s32[4,32]{1,0:T(4,128)} %bitcast.22, ...), custom_call_target="tpu_custom_call" | custom-call | flops 8000000 | bytes 1000000 | tf_op jit(solution)/shard_map/pallas_call | solution.py:514
  41.1 0.7 %shard_map.87 = (f32[4,2,16,256]{3,2,1,0:T(8,128)}, f32[4,8,128]{2,1,0:T(8,128)}) custom-call(f32[4,2,16,256]{3,2,1,0:T(8,128)S(1)} %get-tuple-element.6.iterate, f32[4,8,128]{2,1,0:T(8,128)S(1)} %get-tuple-element.7.coarse), custom_call_target="tpu_custom_call" | custom-call | tf_op jit(solution)/shard_map/pallas_call | solution.py:531
